TPU v7x, 32 devices: a whole 2x2x4 slice. The times are simulated.
32 devices in a mesh: lat: 8 (over z, x), lev: 4 (over y, core).
Axes of the slice: x: 2, y: 2, z: 4, core: 2. Of those that a mesh axis runs over, the one named last changes fastest.
Arguments:
- fields: float32 [2, 32, 64, 3072], P(None, 'lat', 'lev'), may hold values from -6 to 6
- courant: bfloat16 [2, 32, 64, 3072], P(None, 'lat', 'lev'), may hold values from -0.3984375 to 0.3984375
- cutoffs: int32 [32], replicated, may hold values from 1 to 1536, as said below
- surface: float32 [32, 3072], P('lat'), may hold values from -6 to 6
- remap_weights: float32 [64, 64], replicated, may hold values from -0.25 to 0.75
Outputs:
- remapped: float32 [2, 32, 64, 3072], P(None, 'lat', None, 'lev')
- geopotential: float32 [32, 64, 3072], P('lat', None, 'lev')
Inputs may be any that keep to these rules, and one draw needn't show every extreme that they name: cutoffs[j] is 1536 except on the first and the last 4 latitudes, where it lies between 1 and 127; it equals 127 on some latitude among the first 4.
All inputs are finite; a program needn't handle non-finite values.
Results may differ from a plain program's by a relative error of at most 0.0003.
Values may be sent and summed in bfloat16 or wider, within the bound.
No kernel may reach another device: no remote copies, remote signals or barrier semaphores. Data moves between devices by JAX's collectives and lax.ppermute only.
A program may use at most 64 MiB of HBM per device.

v0:
```python
import functools
import math

import jax
import jax.numpy as jnp
import ml_dtypes
import numpy as np
from jax import lax
from jax.experimental import pallas as pl
from jax.experimental.pallas import tpu as pltpu
from jax.sharding import PartitionSpec as P

KMAX = 128
LANE = 128
TOP = 32767.0
STEPS = 256.0
TINY = 2.0**-100
WIND = 81920.0
ROUND = 1.5 * 2.0**23
VMEM_LIMIT = 12 * 2**20
VMEM_MOST = 63 * 2**20 + 2**19


def rounded(values):
    return ((values + ROUND) - ROUND).astype(jnp.int32).astype(jnp.int16)


def lane_max(values):
    chunks = [jnp.abs(values[:, i : i + LANE]) for i in range(0, values.shape[1], LANE)]
    while len(chunks) > 1:
        pairs = [jnp.maximum(a, b) for a, b in zip(chunks[0::2], chunks[1::2])]
        chunks = pairs + chunks[2 * len(pairs) :]
    return chunks[0]


def tiled(tile, width):
    return jnp.concatenate([tile] * (width // LANE), axis=1)


def scale_code(largest):
    return jnp.ceil(jnp.log2(jnp.maximum(largest, TINY)) * STEPS)


def encoder(code):
    return TOP / jnp.exp2(code * (1.0 / STEPS))


def decoder(code16):
    code = code16.astype(jnp.int32).astype(jnp.float32)
    return jnp.exp2(code * (1.0 / STEPS)) * (1.0 / TOP)


def encode_row(values, out_ref, at):
    width = values.shape[1]
    code = scale_code(lane_max(values))
    out_ref[:, at : at + width] = rounded(values * tiled(encoder(code), width))
    out_ref[:, at + width : at + width + LANE] = code.astype(jnp.int32).astype(jnp.int16)


def decode_row(in_ref, at, width):
    scale = decoder(in_ref[:, at + width : at + width + LANE])
    values = in_ref[:, at : at + width].astype(jnp.int32).astype(jnp.float32)
    return values * tiled(scale, width)


def wind_codes(east, north):
    return rounded(jnp.concatenate([east, north], axis=0) * WIND)


class Sizes:
    def __init__(self, rows, levels, lon):
        self.rows, self.levels, self.lon = rows, levels, lon
        self.half = levels // 2
        self.band = 2 * rows
        self.pad = lon + 2 * LANE
        self.code = lon + LANE
        self.edge = 2 * self.code + lon
        self.inner = 2 * self.code + 3 * lon


def put_padded(ref, index, values, lon):
    ref[index + (Ellipsis, slice(LANE, LANE + lon))] = values
    ref[index + (Ellipsis, slice(0, LANE))] = values[..., lon - LANE :]
    ref[index + (Ellipsis, slice(LANE + lon, 2 * LANE + lon))] = values[..., :LANE]


def wind_row(z, wind, upper):
    halves = []
    for k in range(2):
        both = wind[k].astype(jnp.float32)
        halves.append(jnp.where(upper == 1, both[z.half :], both[: z.half]))
    return wind_codes(*halves)


def edge_kernel(z, fields_ref, courant_ref, edge_ref, rows_ref, wind_ref, sems):
    p = lax.rem(lax.axis_index("lat"), 2)
    give = pl.multiple_of((1 - p) * z.half, z.half)
    copies = [
        pltpu.make_async_copy(
            fields_ref.at[f, 2 * p + r, pl.ds(give, z.half)],
            rows_ref.at[r, pl.ds(f * z.half, z.half)],
            sems.at[2 * r + f],
        )
        for r in range(2)
        for f in range(2)
    ]
    copies += [
        pltpu.make_async_copy(courant_ref.at[k, 3 * p], wind_ref.at[k], sems.at[4 + k])
        for k in range(2)
    ]
    for copy in copies:
        copy.start()
    for r in range(2):
        copies[2 * r].wait()
        copies[2 * r + 1].wait()
        encode_row(rows_ref[r], edge_ref, r * z.code)
    copies[4].wait()
    copies[5].wait()
    edge_ref[:, 2 * z.code :] = wind_row(z, wind_ref, 1 - p)


def rest_kernel(z, par_ref, fields_ref, courant_ref, inner_ref, own_ref):
    p = par_ref[0]
    keep = pl.multiple_of(p * z.half, z.half)
    give = pl.multiple_of((1 - p) * z.half, z.half)

    def field_row(row, start):
        return jnp.concatenate([fields_ref[f, row, pl.ds(start, z.half)] for f in range(2)], axis=0)

    def winds(row, upper):
        return wind_row(z, [courant_ref[k, row] for k in range(2)], upper)

    edge, inner = 2 * p, 2 * (1 - p)
    at = 2 * z.code
    for r in range(2):
        encode_row(field_row(inner + r, give), inner_ref, r * z.code)
    for i, row in enumerate((inner, inner + 1, 1 + p)):
        inner_ref[:, at + i * z.lon : at + (i + 1) * z.lon] = winds(row, 1 - p)
    for r in range(2):
        encode_row(field_row(edge + r, keep), own_ref, r * z.code)
    own_ref[:, at : at + z.lon] = winds(3 * p, p)


def shifted(pieces, shift, lanes):
    turned = [pltpu.roll(v, (-shift) % LANE, 1) for v in pieces]
    if shift > 0:
        return [jnp.where(lanes < LANE - shift, a, b) for a, b in zip(turned[1:-1], turned[2:])]
    return [jnp.where(lanes < -shift, a, b) for a, b in zip(turned[:-2], turned[1:-1])]


def substep(z, count_rows, base, row_of, winds_ref, write):
    count = next(n for n in (4, 3, 2, 1) if z.lon % (n * LANE) == 0)
    width = count * LANE
    lanes = lax.broadcasted_iota(jnp.int32, (z.half, LANE), 1)

    def part(i, carry):
        at = pl.multiple_of(i * width, LANE)

        def piece(k):
            return pl.ds(pl.multiple_of(at + k * LANE, LANE), LANE)

        def row(j, f):
            return [row_of(j, f, piece(k + 1)) for k in range(count)]

        def start(j, f):
            pieces = [row_of(j + 2, f, piece(k)) for k in range(count + 2)]
            return [shifted(pieces, s, lanes) for s in (-2, -1, 1, 2)]

        def lon_part(j, u, moved):
            out = []
            for k in range(count):
                m2, m1, p1, p2 = (m[k] for m in moved)
                east = 7.0 * (u[k] + p1) - (m1 + p2)
                west = 7.0 * (m1 + u[k]) - (m2 + p1)
                east = winds_ref[base + j, :, piece(k)] * east
                out.append(east - winds_ref[z.band + base + j, :, piece(k)] * west)
            return out

        for f in range(2):
            rows = [row(j, f) for j in range(4)]
            sums = [[a + b for a, b in zip(rows[j], rows[j + 1])] for j in range(3)]
            flux = None
            moved = start(0, f)
            for j in range(count_rows + 1):
                later = start(j, f) if 0 < j < count_rows else None
                new = [
                    winds_ref[2 * z.band + base + j, :, piece(k)] * (8.0 * sums[1][k] - (sums[0][k] + sums[2][k]))
                    for k in range(count)
                ]
                if j > 0:
                    u = rows[1]
                    change = lon_part(j - 1, u, moved)
                    for k in range(count):
                        write(j - 1, f, at, k, u[k] - change[k] - (new[k] - flux[k]))
                    moved = later
                flux = new
                if j < count_rows:
                    above = row(j + 4, f)
                    rows = rows[1:] + [above]
                    sums = sums[1:] + [[a + b for a, b in zip(rows[2], rows[3])]]
        return carry

    lax.fori_loop(0, z.lon // width, part, 0)


def filter_tables(lon):
    half = lon // 2
    points = np.arange(half)
    forward, back = [], []
    for parity in range(2):
        waves = np.arange(parity, KMAX, 2)
        angle = (points[:, None] * waves[None, :] % lon) * (2.0 * math.pi / lon)
        table = np.concatenate([np.cos(angle), np.sin(angle)], axis=1).astype(np.float32)
        high = table.astype(ml_dtypes.bfloat16)
        low = (table - high.astype(np.float32)).astype(ml_dtypes.bfloat16)
        forward.append(np.concatenate([high, low], axis=1))
        turned = np.concatenate([high.T, low.T], axis=0)
        back.append(np.concatenate(np.split(turned, half // (2 * KMAX), axis=1), axis=0))
    return np.stack(forward + back)


def split(values):
    high = values.astype(jnp.bfloat16)
    return high, (values - high.astype(jnp.float32)).astype(jnp.bfloat16)


def low_pass(z, rows, cuts, table_ref):
    half = z.lon // 2
    count = len(rows)
    tall = 2 * z.half
    total = count * tall
    flat = [row.reshape(tall, z.lon) for row in rows]
    folded = []
    for parity in range(2):
        parts = [
            row[:, :half] + row[:, half:] if parity == 0 else row[:, :half] - row[:, half:]
            for row in flat
        ]
        high, low = split(jnp.concatenate(parts, axis=0))
        both = jnp.concatenate([high, low], axis=0)
        got = jnp.dot(both, table_ref[parity], preferred_element_type=jnp.float32)
        wave = got[:total, :KMAX] + got[:total, KMAX:] + (got[total:, :KMAX] + got[total:, KMAX:])
        number = 2 * (lax.broadcasted_iota(jnp.int32, (tall, KMAX), 1) % (KMAX // 2)) + parity
        doubled = jnp.where(number == 0, 1.0, 2.0) * (1.0 / z.lon)
        weight = jnp.concatenate([jnp.where(number <= cut, doubled, 0.0) for cut in cuts], axis=0)
        high, low = split(wave * weight)
        both = jnp.concatenate(
            [jnp.concatenate([high, high], axis=1), jnp.concatenate([low, low], axis=1)], axis=0
        )
        got = []
        for at in range(0, half, 2 * KMAX):
            block = table_ref[2 + parity, at : at + 2 * KMAX]
            sums = jnp.dot(both, block, preferred_element_type=jnp.float32)
            got.append(sums[:total] + sums[total:])
        folded.append(jnp.concatenate(got, axis=1))
    left, right = folded[0] + folded[1], folded[0] - folded[1]
    smooth = jnp.concatenate([left, right], axis=1)
    return [smooth[i * tall : (i + 1) * tall].reshape(2, z.half, z.lon) for i in range(count)]


def filter_rows(z, cut_ref, first_row, start, table_ref, load, store):
    nyquist = z.lon // 2
    cuts = [cut_ref[first_row + start + r] for r in range(z.rows)]
    some = functools.reduce(jnp.logical_or, [cut < nyquist for cut in cuts])

    @pl.when(some)
    def _():
        smooth = low_pass(z, [load(start + r) for r in range(z.rows)], cuts, table_ref)
        for r in range(z.rows):

            @pl.when(cuts[r] < nyquist)
            def _():
                store(start + r, smooth[r])


def first_kernel(
    z, par_ref, fields_ref, courant_ref, edge_ref, inner_ref, one_ref, two_ref,
    new_ref, winds_ref, one_out_ref, two_out_ref, u_ref, cx_ref, cy_ref,
):
    p, b = par_ref[0], par_ref[3]
    lon, half = z.lon, z.half

    def pair(values):
        return values.reshape(2, half, values.shape[1])

    def winds(in_ref, at):
        values = in_ref[:, at : at + lon].astype(jnp.int32).astype(jnp.float32) * (1.0 / WIND)
        return values[:half], values[half:]

    def place_wind(row, east, north):
        put_padded(cx_ref, (row,), east, lon)
        cy_ref[row + 1] = north

    keep = pl.multiple_of(p * half, half)
    for r in range(z.rows):
        row = z.rows * p + r
        own = jnp.stack([fields_ref[f, r, pl.ds(keep, half)] for f in range(2)])
        put_padded(u_ref, (row + 2,), own, lon)
        got = []
        for k in range(2):
            wind = courant_ref[k, r].astype(jnp.float32)
            got.append(jnp.where(p == 1, wind[half:], wind[:half]))
        place_wind(row, *got)
    at = 2 * z.code
    for r in range(2):
        put_padded(u_ref, (6 * (1 - p) + r + 2,), pair(decode_row(edge_ref, r * z.code, lon)), lon)
        put_padded(u_ref, (4 - 2 * p + r + 2,), pair(decode_row(inner_ref, r * z.code, lon)), lon)
        put_padded(u_ref, (10 * (1 - b) + r,), pair(decode_row(one_ref, r * z.code, lon)), lon)
        put_padded(u_ref, (10 * b + r,), pair(decode_row(two_ref, r * z.code, lon)), lon)
        place_wind(4 - 2 * p + r, *winds(inner_ref, at + r * lon))
    place_wind(7 * (1 - p), *winds(edge_ref, at))
    place_wind(6 - 5 * p, *winds(inner_ref, at + 2 * lon))
    cy_ref[9 * (1 - b)] = winds(one_ref, at)[1]
    cy_ref[9 * b] = winds(two_ref, at)[1]

    def face_rows(j, carry):
        wind = cx_ref[j] * (1.0 / 24.0)
        here = wind[:, LANE : LANE + lon]
        winds_ref[j] = here + pltpu.roll(wind, z.pad - 1, 1)[:, LANE : LANE + lon]
        winds_ref[z.band + j] = here + pltpu.roll(wind, 1, 1)[:, LANE : LANE + lon]
        return carry

    lax.fori_loop(0, z.band, face_rows, 0)

    def face_cols(j, carry):
        winds_ref[2 * z.band + j] = (cy_ref[j] + cy_ref[j + 1]) * (1.0 / 24.0)
        return carry

    lax.fori_loop(0, z.band + 1, face_cols, 0)

    def write(row, f, at, k, values):
        new_ref[row, f, :, pl.ds(pl.multiple_of(at + (k + 1) * LANE, LANE), LANE)] = values

    substep(z, z.band, 0, lambda j, f, piece: u_ref[j, f, :, piece], winds_ref, write)
    for r in range(2):
        for row, out_ref in ((6 * (1 - b) + r, one_out_ref), (6 * b + r, two_out_ref)):
            values = new_ref[row, :, :, LANE : LANE + lon]
            encode_row(values.reshape(2 * half, lon), out_ref, r * z.code)
    for j in range(z.band):
        new_ref[j, :, :, 0:LANE] = new_ref[j, :, :, lon : lon + LANE]
        new_ref[j, :, :, LANE + lon :] = new_ref[j, :, :, LANE : 2 * LANE]


def inner_kernel(z, par_ref, cut_ref, in_ref, winds_ref, table_ref, new_ref, inner_ref):
    for j in range(z.band):
        new_ref[j] = in_ref[j]

    def store(row, values):
        put_padded(new_ref, (row,), values, z.lon)

    for part in range(2):
        filter_rows(
            z, cut_ref, par_ref[1], part * z.rows, table_ref,
            lambda row: in_ref[row, :, :, LANE : LANE + z.lon], store,
        )

    def write(row, f, at, k, values):
        inner_ref[row, f, :, pl.ds(pl.multiple_of(at + k * LANE, LANE), LANE)] = values

    substep(z, z.band - 4, 2, lambda j, f, piece: new_ref[j, f, :, piece], winds_ref, write)


def outer_kernel(
    z, parts, partner, par_ref, cut_ref, new_ref, inner_ref, winds_ref, one_ref, two_ref, table_ref, *refs
):
    refs = refs if partner else refs[1:]
    out_refs, (u_ref, v_ref) = refs[:parts], refs[parts:]
    lon, half = z.lon, z.half
    tall = 2 * half
    side = 1 - par_ref[0] if partner else par_ref[0]
    base = z.rows * side

    def halo(in_ref):
        for r in range(2):
            values = decode_row(in_ref, r * z.code, lon).reshape(2, half, lon)
            put_padded(u_ref, (4 * side + r,), values, lon)

    first_swap = side + par_ref[3] == 1
    pl.when(first_swap)(lambda: halo(one_ref))
    pl.when(jnp.logical_not(first_swap))(lambda: halo(two_ref))
    for r in range(4):
        u_ref[2 * (1 - side) + r] = new_ref[base + r]
    for r in range(2):
        v_ref[2 * (1 - side) + r] = inner_ref[2 * side + r]

    def write(row, f, at, k, values):
        v_ref[2 * side + row, f, :, pl.ds(pl.multiple_of(at + k * LANE, LANE), LANE)] = values

    substep(z, 2, 6 * side, lambda j, f, piece: u_ref[j, f, :, piece], winds_ref, write)

    def store(row, values):
        v_ref[row] = values

    filter_rows(z, cut_ref, par_ref[1] + base, 0, table_ref, lambda row: v_ref[row], store)
    column = lon // parts
    for b in range(parts):
        at = pl.multiple_of(jnp.bitwise_xor(par_ref[2], b) * column, LANE)
        values = jnp.concatenate(
            [v_ref[r, :, :, pl.ds(at, column)].reshape(tall, column) for r in range(z.rows)], axis=1
        )
        encode_row(values, out_refs[b], 0)


def scale_kernel(at, *refs):
    for i, ref in enumerate(refs[:-1]):
        refs[-1][i] = decoder(ref[:, at : at + LANE])


def column_kernel(z, parts, par_ref, *refs):
    got, (scales_ref, remap_ref, upward_ref, surface_ref, out_ref, geo_ref, x_ref) = refs[: 2 * parts], refs[2 * parts :]
    p, lev = par_ref[0], par_ref[2]
    column = out_ref.shape[-1]
    at = pl.multiple_of(pl.program_id(0) * column, LANE)
    for i, ref in enumerate(got):
        side = p if i < parts else 1 - p
        s = jnp.bitwise_xor(lev, i % parts)
        if i < parts:
            scale = decoder(ref[:, z.rows * column : z.rows * column + LANE])
        else:
            scale = scales_ref[i - parts]
        codes = ref[:, pl.ds(at, column)].astype(jnp.int32).astype(jnp.float32)
        values = codes * tiled(scale, column)
        level = pl.multiple_of(s * z.levels + side * z.half, z.half)
        for f in range(2):
            x_ref[f, pl.ds(level, z.half)] = values[f * z.half : (f + 1) * z.half]
    high, low = split(remap_ref[...])
    remap = jnp.concatenate([high, low, high], axis=1)
    count = remap_ref.shape[0]
    for f in range(2):
        high, low = split(x_ref[f])
        stacked = jnp.concatenate([high, high, low], axis=0)
        left = remap if f == 0 else jnp.concatenate([remap, upward_ref[...].astype(jnp.bfloat16)], axis=0)
        result = jnp.dot(left, stacked, preferred_element_type=jnp.float32)
        out_ref[f, 0] = result[:count]
        if f == 1:
            geo_ref[0] = surface_ref[0] + result[count:] * (count**-0.5)


def whole():
    return pl.BlockSpec(memory_space=pltpu.VMEM)


def scalars():
    return pl.BlockSpec(memory_space=pltpu.SMEM)


def far_memory():
    return pl.BlockSpec(memory_space=pltpu.HBM)


def params(limit=VMEM_LIMIT):
    return pltpu.CompilerParams(vmem_limit_bytes=limit)


def cost(flops=1000, data=1000):
    return pl.CostEstimate(flops=flops, bytes_accessed=data, transcendentals=0)


def shards(fields, courant, cutoffs, surface, remap_weights):
    _, rows, levels, lon = fields.shape
    z = Sizes(rows, levels, lon)
    lats, parts = lax.axis_size("lat"), lax.axis_size("lev")
    me = lax.axis_index("lat")
    parity = me % 2
    lev = lax.axis_index("lev")
    place = jnp.stack([parity, (me - parity) * rows, lev, (me // 2) % 2]).astype(jnp.int32)
    tall = 2 * z.half
    i16, f32 = jnp.int16, jnp.float32
    swap = [(i, i ^ 1) for i in range(lats)]
    ones, twos = [
        [pair for i in range(start, lats - 2, 4) for s in range(2) for pair in ((i + s, i + s + 2), (i + s + 2, i + s))]
        for start in (0, 2)
    ]

    def shape(*dims):
        return jax.ShapeDtypeStruct(dims, f32)

    def codes(*dims):
        return jax.ShapeDtypeStruct(dims, i16)

    edge = pl.pallas_call(
        functools.partial(edge_kernel, z),
        name="edge",
        in_specs=[far_memory(), far_memory()],
        out_specs=whole(),
        out_shape=codes(tall, z.edge),
        scratch_shapes=[
            pltpu.VMEM((2, tall, lon), f32),
            pltpu.VMEM((2, levels, lon), courant.dtype),
            pltpu.SemaphoreType.DMA((6,)),
        ],
        compiler_params=params(VMEM_MOST),
        cost_estimate=cost(),
    )(fields, courant)
    edge = lax.ppermute(edge, "lat", swap)
    inner, own = pl.pallas_call(
        functools.partial(rest_kernel, z),
        name="rest",
        in_specs=[scalars(), whole(), whole()],
        out_specs=[whole()] * 2,
        out_shape=[codes(tall, z.inner), codes(tall, z.edge)],
        compiler_params=params(),
        cost_estimate=cost(),
    )(place, fields, courant)
    inner = lax.ppermute(inner, "lat", swap)
    straight = (parity + (me // 2) % 2) == 1
    one = lax.ppermute(jnp.where(straight, own, edge), "lat", ones)
    two = lax.ppermute(jnp.where(straight, edge, own), "lat", twos)
    new, winds, one_code, two_code = pl.pallas_call(
        functools.partial(first_kernel, z),
        name="first",
        in_specs=[scalars()] + [whole()] * 6,
        out_specs=[whole()] * 4,
        out_shape=[
            shape(z.band, 2, z.half, z.pad),
            shape(3 * z.band + 1, z.half, lon),
            codes(tall, 2 * z.code),
            codes(tall, 2 * z.code),
        ],
        scratch_shapes=[
            pltpu.VMEM((z.band + 4, 2, z.half, z.pad), f32),
            pltpu.VMEM((z.band, z.half, z.pad), f32),
            pltpu.VMEM((z.band + 2, z.half, z.lon), f32),
        ],
        compiler_params=params(),
        cost_estimate=cost(),
    )(place, fields, courant, edge, inner, one, two)
    one = lax.ppermute(one_code, "lat", ones)
    two = lax.ppermute(two_code, "lat", twos)

    tables = jnp.asarray(filter_tables(lon))
    new, inner = pl.pallas_call(
        functools.partial(inner_kernel, z),
        name="inner",
        in_specs=[scalars(), scalars()] + [whole()] * 3,
        out_specs=[whole()] * 2,
        out_shape=[shape(z.band, 2, z.half, z.pad), shape(z.band - 4, 2, z.half, lon)],
        compiler_params=params(),
        cost_estimate=cost(),
    )(place, cutoffs, new, winds, tables)

    column = lon // parts

    def outer(*after):
        partner = not after
        return pl.pallas_call(
            functools.partial(outer_kernel, z, parts, partner),
            name="outer_partner" if partner else "outer_own",
            in_specs=[scalars(), scalars()] + [whole()] * 6 + [far_memory()] * len(after),
            out_specs=[whole()] * parts,
            out_shape=[codes(tall, rows * column + LANE)] * parts,
            scratch_shapes=[
                pltpu.VMEM((6, 2, z.half, z.pad), f32),
                pltpu.VMEM((z.rows, 2, z.half, lon), f32),
            ],
            compiler_params=params(),
            cost_estimate=cost(),
        )(place, cutoffs, new, inner, winds, one, two, tables, *after)

    blocks = outer()
    got = []
    for b, block in enumerate(blocks):
        pairs = [
            (i * parts + j, (i ^ 1) * parts + (j ^ b)) for i in range(lats) for j in range(parts)
        ]
        got.append(lax.ppermute(block, ("lat", "lev"), pairs))
    scales = pl.pallas_call(
        functools.partial(scale_kernel, rows * column),
        name="scales",
        in_specs=[whole()] * parts,
        out_specs=whole(),
        out_shape=shape(parts, tall, LANE),
        compiler_params=params(),
        cost_estimate=cost(),
    )(*got)
    for b, block in enumerate(outer(blocks[0])):
        pairs = [(j, j ^ b) for j in range(parts)]
        got.insert(b, lax.ppermute(block, "lev", pairs) if b else block)

    count = remap_weights.shape[0]
    upward = np.triu(np.ones((count, count), np.float32), 1) + 0.5 * np.eye(count, dtype=np.float32)
    upward = jnp.asarray(np.concatenate([upward, 0.0 * upward, upward], axis=1))
    surface = lax.dynamic_slice_in_dim(surface, lev * column, column, 1)
    remapped, geopotential = pl.pallas_call(
        functools.partial(column_kernel, z, parts),
        name="columns",
        grid=(rows,),
        in_specs=[scalars()]
        + [whole()] * (len(got) + 1)
        + [
            pl.BlockSpec(remap_weights.shape, lambda r: (0, 0)),
            pl.BlockSpec(upward.shape, lambda r: (0, 0)),
            pl.BlockSpec((1, 1, column), lambda r: (r, 0, 0)),
        ],
        out_specs=[
            pl.BlockSpec((2, 1, count, column), lambda r: (0, r, 0, 0)),
            pl.BlockSpec((1, count, column), lambda r: (r, 0, 0)),
        ],
        out_shape=[shape(2, rows, count, column), shape(rows, count, column)],
        scratch_shapes=[pltpu.VMEM((2, count, column), f32)],
        compiler_params=params(),
        cost_estimate=cost(),
    )(place, *got, scales, remap_weights, upward, surface[:, None, :])
    return remapped, geopotential


def with_halo(shard, width):
    size, length = lax.axis_size("lat"), shard.shape[1]
    up = [(i, (i + 1) % size) for i in range(size - 1)]
    down = [(j, i) for i, j in up]
    before = lax.ppermute(lax.slice_in_dim(shard, length - width, length, axis=1), "lat", up)
    after = lax.ppermute(lax.slice_in_dim(shard, 0, width, axis=1), "lat", down)
    return jnp.concatenate([before, shard, after], axis=1)


def plain_shards(fields, courant, cutoffs, surface, remap_weights):
    _, rows, _, lon = fields.shape
    exact = lax.Precision.HIGHEST
    cut = lax.dynamic_slice_in_dim(cutoffs, lax.axis_index("lat") * rows, rows)
    waves = np.arange(KMAX)
    angle = (np.arange(lon)[:, None] * waves[None, :] % lon) * (2.0 * math.pi / lon)
    table = jnp.asarray(np.concatenate([np.cos(angle), np.sin(angle)], axis=1).astype(np.float32))
    number = jnp.asarray(np.concatenate([waves, waves]).astype(np.int32))
    weight = jnp.where(number[None] <= cut[:, None], jnp.where(number == 0, 1.0, 2.0)[None] / lon, 0.0)
    flagged = cut < lon // 2

    def smooth(values):
        wave = jnp.einsum("frln,nk->frlk", values, table, precision=exact) * weight[None, :, None]
        low = jnp.einsum("frlk,nk->frln", wave, table, precision=exact)
        return jnp.where(flagged[None, :, None, None], low, values)

    winds = with_halo(courant, 1).astype(jnp.float32)
    east, north = winds[0, 1:-1], winds[1]
    face_x = (east + jnp.roll(east, -1, -1)) / 24.0
    face_y = (north[:-1] + north[1:]) / 24.0
    u = fields
    for _ in range(2):
        wide = with_halo(u, 2)
        pair = u + jnp.roll(u, -1, -1)
        fx = face_x * (8.0 * pair - (jnp.roll(pair, 1, -1) + jnp.roll(pair, -1, -1)))
        pair = wide[:, :-1] + wide[:, 1:]
        fy = face_y * (8.0 * pair[:, 1:-1] - (pair[:, :-2] + pair[:, 2:]))
        u = u - (fx - jnp.roll(fx, 1, -1)) - (fy[:, 1:] - fy[:, :-1])
        u = lax.cond(jnp.any(flagged), smooth, lambda values: values, u)
    columns = lax.all_to_all(u, "lev", split_axis=3, concat_axis=2, tiled=True)
    remapped = jnp.einsum("pk,fjkn->fjpn", remap_weights, columns, precision=exact)
    count = remap_weights.shape[0]
    upward = np.triu(np.ones((count, count), np.float32), 1) + 0.5 * np.eye(count, dtype=np.float32)
    upward = jnp.einsum("kl,jln->jkn", jnp.asarray(upward), columns[1], precision=exact)
    width = lon // lax.axis_size("lev")
    mine = lax.dynamic_slice_in_dim(surface, lax.axis_index("lev") * width, width, 1)
    return remapped, mine[:, None] + count**-0.5 * upward


def solution(mesh):
    def program(fields, courant, cutoffs, surface, remap_weights):
        lats, parts = mesh.shape["lat"], mesh.shape["lev"]
        rows, levels = fields.shape[1] // lats, fields.shape[2] // parts
        polar = fields.shape[1] // 8
        paired = (
            lats % 2 == 0
            and rows == 4
            and levels % 16 == 0
            and polar <= 2 * rows - 2
            and fields.shape[3] % (LANE * parts) == 0
            and parts & (parts - 1) == 0
            and fields.shape[3] % (4 * KMAX) == 0
        )
        return jax.shard_map(
            shards if paired else plain_shards,
            mesh=mesh,
            in_specs=(
                P(None, "lat", "lev", None),
                P(None, "lat", "lev", None),
                P(),
                P("lat", None),
                P(),
            ),
            out_specs=(P(None, "lat", None, "lev"), P("lat", None, "lev")),
            check_vma=False,
        )(fields, courant, cutoffs, surface, remap_weights)

    return program
```

profile of v0, /device:TPU:17, one launch (start us, length us, event | category | flops | bytes accessed | tf_op | source)
XLA Modules:
  0.0 64.4 jit_solution(5535243438578516739)
XLA Ops:
  0.6 0.0 copy-start
  0.6 2.0 %edge.1 = s16[16,9472]{1,0:T(8,128)(2,1)} custom-call(f32[2,4,16,3072]{3,2,1,0:T(8,128)} %fields_ref.5, bf16[2,4,16,3072]{3,2,1,0:T(8,128)(2,1)} %courant_ref.5), custom_call_target="tpu_custom_call" | custom-call | flops 1000 | bytes 1000 | tf_op jit(solution)/shard_map/edge/pallas_call | solution.py:481
  2.6 1.3 %collective-permute-start = (s16[16,9472]{1,0:T(8,128)(2,1)}, s16[16,9472]{1,0:T(8,128)(2,1)S(1)}, u32[]{:S(2)}, u32[]{:S(2)}) collective-permute-start(s16[16,9472]{1,0:T(8,128)(2,1)} %edge.1), channel_id=1, source_target_pairs={{0,4},{4,0},{8,12},{12,8},{16,20},{20,16},{24,28},{28,24},{1,5},{5... | collective-permute-start | bytes 909320 | tf_op jit(solution)/shard_map/ppermute | solution.py:495
  3.9 0.1 pad_add_fusion.par_ref
  4.0 1.4 %copy-done.3 = f32[2,4,16,3072]{3,2,1,0:T(8,128)S(1)} copy-done((f32[2,4,16,3072]{3,2,1,0:T(8,128)S(1)}, f32[2,4,16,3072]{3,2,1,0:T(8,128)}, u32[]{:S(2)}) %copy-start.3) | copy-done | bytes 1572888
  5.4 1.1 %copy-done.5 = bf16[2,4,16,3072]{3,2,1,0:T(8,128)(2,1)S(1)} copy-done((bf16[2,4,16,3072]{3,2,1,0:T(8,128)(2,1)S(1)}, bf16[2,4,16,3072]{3,2,1,0:T(8,128)(2,1)}, u32[]{:S(2)}) %copy-start.5) | copy-done | bytes 786456
  6.5 1.0 %rest.1 = (s16[16,15616]{1,0:T(8,128)(2,1)S(1)}, s16[16,9472]{1,0:T(8,128)(2,1)S(1)}) custom-call(s32[4]{0:T(128)S(1)} %pad_add_fusion.par_ref, f32[2,4,16,3072]{3,2,1,0:T(8,128)S(1)} %copy-done.3, bf16[2,4,16,3072]{3,2,1,0:T(8,128)(2,1)S(1)} %copy-done.5), custom_call_target="tpu_custom_call" | custom-call | flops 1000 | bytes 1000 | tf_op jit(solution)/shard_map/rest/pallas_call | solution.py:496
  7.5 0.3 collective-permute-start.1
  7.8 3.1 %collective-permute-done.edge_ref = s16[16,9472]{1,0:T(8,128)(2,1)S(1)} collective-permute-done((s16[16,9472]{1,0:T(8,128)(2,1)}, s16[16,9472]{1,0:T(8,128)(2,1)S(1)}, u32[]{:S(2)}, u32[]{:S(2)}) %collective-permute-start) | collective-permute-done | bytes 303136 | tf_op jit(solution)/shard_map/ppermute | solution.py:495
  11.0 0.1 broadcast_select_fusion
  11.1 1.4 %collective-permute-start.2 = (s16[16,9472]{1,0:T(8,128)(2,1)S(1)}, s16[16,9472]{1,0:T(8,128)(2,1)S(1)}, u32[]{:S(2)}, u32[]{:S(2)}) collective-permute-start(s16[16,9472]{1,0:T(8,128)(2,1)S(1)} %get-tuple-element.35), channel_id=1, source_target_pairs={{0,8},{8,0},{4,12},{12,4},{16,24},{24,16},{20,28},{28,20},{1,9},{9... | collective-permute-start | bytes 909320 | tf_op jit(solution)/shard_map/ppermute | solution.py:507
  12.4 2.2 %collective-permute-start.3 = (s16[16,9472]{1,0:T(8,128)(2,1)S(1)}, s16[16,9472]{1,0:T(8,128)(2,1)S(1)}, u32[]{:S(2)}, u32[]{:S(2)}) collective-permute-start(s16[16,9472]{1,0:T(8,128)(2,1)S(1)} %get-tuple-element.34), channel_id=1, source_target_pairs={{8,16},{16,8},{12,20},{20,12},{9,17},{17,9},{13,21},{21,13},{10,18... | collective-permute-start | bytes 909320 | tf_op jit(solution)/shard_map/ppermute | solution.py:508
  14.6 7.1 %collective-permute-done.1.inner_ref = s16[16,15616]{1,0:T(8,128)(2,1)S(1)} collective-permute-done((s16[16,15616]{1,0:T(8,128)(2,1)S(1)}, s16[16,15616]{1,0:T(8,128)(2,1)S(1)}, u32[]{:S(2)}, u32[]{:S(2)}) %collective-permute-start.1) | collective-permute-done | bytes 499744 | tf_op jit(solution)/shard_map/ppermute | solution.py:505
  21.7 0.8 %copy-done.11 = s16[16,15616]{1,0:T(8,128)(2,1)} copy-done((s16[16,15616]{1,0:T(8,128)(2,1)}, s16[16,15616]{1,0:T(8,128)(2,1)S(1)}, u32[]{:S(2)}) %copy-start.11) | copy-done | bytes 499736
  22.4 0.0 collective-permute-done.2.one_ref
  22.4 0.0 collective-permute-done.3.two_ref
  22.5 1.4 %copy-done.4 = f32[2,4,16,3072]{3,2,1,0:T(8,128)S(1)} copy-done((f32[2,4,16,3072]{3,2,1,0:T(8,128)S(1)}, f32[2,4,16,3072]{3,2,1,0:T(8,128)}, u32[]{:S(2)}) %copy-start.4) | copy-done | bytes 1572888
  23.9 1.1 %copy-done.6 = bf16[2,4,16,3072]{3,2,1,0:T(8,128)(2,1)S(1)} copy-done((bf16[2,4,16,3072]{3,2,1,0:T(8,128)(2,1)S(1)}, bf16[2,4,16,3072]{3,2,1,0:T(8,128)(2,1)}, u32[]{:S(2)}) %copy-start.6) | copy-done | bytes 786456
  25.0 1.0 %copy-done.12 = s16[16,15616]{1,0:T(8,128)(2,1)S(1)} copy-done((s16[16,15616]{1,0:T(8,128)(2,1)S(1)}, s16[16,15616]{1,0:T(8,128)(2,1)}, u32[]{:S(2)}) %copy-start.12) | copy-done | bytes 499736
  26.0 4.8 %first.1 = (f32[8,2,8,3328]{3,2,1,0:T(8,128)S(1)}, f32[25,8,3072]{2,1,0:T(8,128)S(1)}, s16[16,6400]{1,0:T(8,128)(2,1)S(1)}, s16[16,6400]{1,0:T(8,128)(2,1)S(1)}) custom-call(s32[4]{0:T(128)S(1)} %pad_add_fusion.par_ref, f32[2,4,16,3072]{3,2,1,0:T(8,128)S(1)} %copy-done.4, bf16[2,4,16,3072]{3,2,1,0:T(8,128)(2,1)S(1)} %copy-done.6, ...), custom_call_target="tpu_custom_call" | custom-call | flops 1000 | bytes 1000 | tf_op jit(solution)/shard_map/first/pallas_call | solution.py:509
  30.8 1.4 %collective-permute-start.4 = (s16[16,6400]{1,0:T(8,128)(2,1)S(1)}, s16[16,6400]{1,0:T(8,128)(2,1)S(1)}, u32[]{:S(2)}, u32[]{:S(2)}) collective-permute-start(s16[16,6400]{1,0:T(8,128)(2,1)S(1)} %get-tuple-element.24), channel_id=1, source_target_pairs={{0,8},{8,0},{4,12},{12,4},{16,24},{24,16},{20,28},{28,20},{1,9},{9... | collective-permute-start | bytes 614408 | tf_op jit(solution)/shard_map/ppermute | solution.py:528
  32.2 1.9 %collective-permute-start.5 = (s16[16,6400]{1,0:T(8,128)(2,1)S(1)}, s16[16,6400]{1,0:T(8,128)(2,1)S(1)}, u32[]{:S(2)}, u32[]{:S(2)}) collective-permute-start(s16[16,6400]{1,0:T(8,128)(2,1)S(1)} %get-tuple-element.25), channel_id=1, source_target_pairs={{8,16},{16,8},{12,20},{20,12},{9,17},{17,9},{13,21},{21,13},{10,18... | collective-permute-start | bytes 614408 | tf_op jit(solution)/shard_map/ppermute | solution.py:529
  34.1 2.1 %inner.1 = (f32[8,2,8,3328]{3,2,1,0:T(8,128)S(1)}, f32[4,2,8,3072]{3,2,1,0:T(8,128)S(1)}) custom-call(s32[4]{0:T(128)S(1)} %pad_add_fusion.par_ref, s32[32]{0:T(128)S(1)} %copy-done.15, f32[8,2,8,3328]{3,2,1,0:T(8,128)S(1)} %get-tuple-element.20.in_ref, f32[25,8,3072]{2,1,0:T(8,128)S(1)} %get-tuple-element.21.winds_ref, bf16[4,1536,256]{2,1,0:T(8,128)(2,1)S(1)} %copy-done.1), custom_call_target="tpu_custom_call" | custom-call | flops 1000 | bytes 1000 | tf_op jit(solution)/shard_map/inner/pallas_call | solution.py:532
  36.3 0.0 copy-start.9
  36.3 0.0 collective-permute-done.4.one_ref
  36.3 2.4 %collective-permute-done.5.two_ref = s16[16,6400]{1,0:T(8,128)(2,1)S(1)} collective-permute-done((s16[16,6400]{1,0:T(8,128)(2,1)S(1)}, s16[16,6400]{1,0:T(8,128)(2,1)S(1)}, u32[]{:S(2)}, u32[]{:S(2)}) %collective-permute-start.5) | collective-permute-done | bytes 204832 | tf_op jit(solution)/shard_map/ppermute | solution.py:529
  38.7 1.9 %outer_partner.1 = (s16[16,3200]{1,0:T(8,128)(2,1)S(1)}, s16[16,3200]{1,0:T(8,128)(2,1)S(1)}, s16[16,3200]{1,0:T(8,128)(2,1)S(1)}, s16[16,3200]{1,0:T(8,128)(2,1)S(1)}) custom-call(s32[4]{0:T(128)S(1)} %pad_add_fusion.par_ref, s32[32]{0:T(128)S(1)} %copy-done.15, f32[8,2,8,3328]{3,2,1,0:T(8,128)S(1)} %get-tuple-element.22.new_ref, ...), custom_call_target="tpu_custom_call" | custom-call | flops 1000 | bytes 1000 | tf_op jit(solution)/shard_map/outer_partner/pallas_call | solution.py:546
  40.5 0.0 copy-done.7
  40.5 0.0 copy-done.9
  40.6 4.1 %collective-permute-start.10 = (s16[16,3200]{1,0:T(8,128)(2,1)S(1)}, s16[16,3200]{1,0:T(8,128)(2,1)S(1)}, u32[]{:S(2)}, u32[]{:S(2)}) collective-permute-start(s16[16,3200]{1,0:T(8,128)(2,1)S(1)} %get-tuple-element.31), channel_id=1, source_target_pairs={{0,5},{1,4},{2,7},{3,6},{4,1},{5,0},{6,3},{7,2},{8,13},{9,12},{10,... | collective-permute-start | bytes 307208 | tf_op jit(solution)/shard_map/ppermute | solution.py:566
  44.7 1.2 %collective-permute-start.11 = (s16[16,3200]{1,0:T(8,128)(2,1)S(1)}, s16[16,3200]{1,0:T(8,128)(2,1)S(1)}, u32[]{:S(2)}, u32[]{:S(2)}) collective-permute-start(s16[16,3200]{1,0:T(8,128)(2,1)S(1)} %get-tuple-element.32), channel_id=1, source_target_pairs={{0,6},{1,7},{2,4},{3,5},{4,2},{5,3},{6,0},{7,1},{8,14},{9,15},{10,... | collective-permute-start | bytes 307208 | tf_op jit(solution)/shard_map/ppermute | solution.py:566
  45.9 0.3 collective-permute-start.12
  46.2 1.2 %collective-permute-start.9 = (s16[16,3200]{1,0:T(8,128)(2,1)S(1)}, s16[16,3200]{1,0:T(8,128)(2,1)S(1)}, u32[]{:S(2)}, u32[]{:S(2)}) collective-permute-start(s16[16,3200]{1,0:T(8,128)(2,1)S(1)} %get-tuple-element.26.refs_0_), channel_id=1, source_target_pairs={{0,4},{1,5},{2,6},{3,7},{4,0},{5,1},{6,2},{7,3},{8,12},{9,13},{10,... | collective-permute-start | bytes 307208 | tf_op jit(solution)/shard_map/ppermute | solution.py:566
  47.4 1.9 %copy-done.2 = bf16[4,1536,256]{2,1,0:T(8,128)(2,1)S(1)} copy-done((bf16[4,1536,256]{2,1,0:T(8,128)(2,1)S(1)}, bf16[4,1536,256]{2,1,0:T(8,128)(2,1)}, u32[]{:S(2)}) %copy-start.2) | copy-done | bytes 3145752
  49.3 1.5 %copy-done.8 = f32[8,2,8,3328]{3,2,1,0:T(8,128)S(1)} copy-done((f32[8,2,8,3328]{3,2,1,0:T(8,128)S(1)}, f32[8,2,8,3328]{3,2,1,0:T(8,128)}, u32[]{:S(2)}) %copy-start.8) | copy-done | bytes 1703960
  50.8 1.1 %copy-done.10 = f32[4,2,8,3072]{3,2,1,0:T(8,128)S(1)} copy-done((f32[4,2,8,3072]{3,2,1,0:T(8,128)S(1)}, f32[4,2,8,3072]{3,2,1,0:T(8,128)}, u32[]{:S(2)}) %copy-start.10) | copy-done | bytes 786456
  51.9 1.9 %outer_own.1 = (s16[16,3200]{1,0:T(8,128)(2,1)S(1)}, s16[16,3200]{1,0:T(8,128)(2,1)S(1)}, s16[16,3200]{1,0:T(8,128)(2,1)S(1)}, s16[16,3200]{1,0:T(8,128)(2,1)S(1)}) custom-call(s32[4]{0:T(128)S(1)} %pad_add_fusion.par_ref, s32[32]{0:T(128)S(1)} %copy-done.15, f32[8,2,8,3328]{3,2,1,0:T(8,128)S(1)} %copy-done.8, f32[4,2,8,3072]{3,2,1,0:T(8,128)S(1)} %copy-done.10, ...), custom_call_target="tpu_custom_call" | custom-call | flops 1000 | bytes 1000 | tf_op jit(solution)/shard_map/outer_own/pallas_call | solution.py:546
  53.8 0.6 collective-permute-start.6
  54.4 0.0 collective-permute-done.10.refs_1_.refs_5_
  54.4 1.3 %collective-permute-start.7 = (s16[16,3200]{1,0:T(8,128)(2,1)S(1)}, s16[16,3200]{1,0:T(8,128)(2,1)S(1)}, u32[]{:S(2)}, u32[]{:S(2)}) collective-permute-start(s16[16,3200]{1,0:T(8,128)(2,1)S(1)} %get-tuple-element.29), channel_id=1, source_target_pairs={{0,2},{1,3},{2,0},{3,1},{4,6},{5,7},{6,4},{7,5},{8,10},{9,11},{10,... | collective-permute-start | bytes 307208 | tf_op jit(solution)/shard_map/ppermute | solution.py:578
  55.7 0.0 collective-permute-done.11.refs_2_.refs_6_
  55.7 0.5 collective-permute-start.8
  56.2 0.0 collective-permute-done.12.refs_3_.refs_7_
  56.2 0.0 collective-permute-done.9.refs_0_.refs_4_
  56.2 0.0 collective-permute-done.6.refs_1_
  56.2 2.7 %collective-permute-done.7.refs_2_ = s16[16,3200]{1,0:T(8,128)(2,1)S(1)} collective-permute-done((s16[16,3200]{1,0:T(8,128)(2,1)S(1)}, s16[16,3200]{1,0:T(8,128)(2,1)S(1)}, u32[]{:S(2)}, u32[]{:S(2)}) %collective-permute-start.7) | collective-permute-done | bytes 102432 | tf_op jit(solution)/shard_map/ppermute | solution.py:578
  58.9 2.4 %collective-permute-done.8.refs_3_ = s16[16,3200]{1,0:T(8,128)(2,1)S(1)} collective-permute-done((s16[16,3200]{1,0:T(8,128)(2,1)S(1)}, s16[16,3200]{1,0:T(8,128)(2,1)S(1)}, u32[]{:S(2)}, u32[]{:S(2)}) %collective-permute-start.8) | collective-permute-done | bytes 102432 | tf_op jit(solution)/shard_map/ppermute | solution.py:578
  61.2 3.2 %columns.1 = (f32[2,4,64,768]{3,2,1,0:T(8,128)}, f32[4,64,768]{2,1,0:T(8,128)}) custom-call(s32[4]{0:T(128)S(1)} %pad_add_fusion.par_ref, s16[16,3200]{1,0:T(8,128)(2,1)S(1)} %get-tuple-element.27.refs_0_, s16[16,3200]{1,0:T(8,128)(2,1)S(1)} %collective-permute-done.6.refs_1_, s16[16,3200]{1,0:T(8,128)(2,1)S(1)} %collective-permute-done.7.refs_2_, ...), custom_call_target="tpu_custom_call" | custom-call | flops 1000 | bytes 1000 | tf_op jit(solution)/shard_map/columns/pallas_call | solution.py:584
  (22 shorter events, 0.1 us)
Async XLA Ops:
  0.6 55.5 %copy-start = (f32[4,3072]{1,0:T(4,128)S(1)}, f32[4,3072]{1,0:T(4,128)}, u32[]{:S(2)}) copy-start(f32[4,3072]{1,0:T(4,128)} %param.10) | copy-start | bytes 147460
  2.6 8.3 %collective-permute-start = (s16[16,9472]{1,0:T(8,128)(2,1)}, s16[16,9472]{1,0:T(8,128)(2,1)S(1)}, u32[]{:S(2)}, u32[]{:S(2)}) collective-permute-start(s16[16,9472]{1,0:T(8,128)(2,1)} %edge.1), channel_id=1, source_target_pairs={{0,4},{4,0},{8,12},{12,8},{16,20},{20,16},{24,28},{28,24},{1,5},{5... | collective-permute-start | bytes 909320 | tf_op jit(solution)/shard_map/ppermute | solution.py:495
  4.0 1.4 %copy-start.3 = (f32[2,4,16,3072]{3,2,1,0:T(8,128)S(1)}, f32[2,4,16,3072]{3,2,1,0:T(8,128)}, u32[]{:S(2)}) copy-start(f32[2,4,16,3072]{3,2,1,0:T(8,128)} %fields_ref.5) | copy-start | bytes 4718596
  5.4 1.1 %copy-start.5 = (bf16[2,4,16,3072]{3,2,1,0:T(8,128)(2,1)S(1)}, bf16[2,4,16,3072]{3,2,1,0:T(8,128)(2,1)}, u32[]{:S(2)}) copy-start(bf16[2,4,16,3072]{3,2,1,0:T(8,128)(2,1)} %courant_ref.5) | copy-start | bytes 2359300
  7.5 14.2 %collective-permute-start.1 = (s16[16,15616]{1,0:T(8,128)(2,1)S(1)}, s16[16,15616]{1,0:T(8,128)(2,1)S(1)}, u32[]{:S(2)}, u32[]{:S(2)}) collective-permute-start(s16[16,15616]{1,0:T(8,128)(2,1)S(1)} %get-tuple-element.18), channel_id=1, source_target_pairs={{0,4},{4,0},{8,12},{12,8},{16,20},{20,16},{24,28},{28,24},{1,5},{5... | collective-permute-start | bytes 1499144 | tf_op jit(solution)/shard_map/ppermute | solution.py:505
  11.1 11.4 %collective-permute-start.2 = (s16[16,9472]{1,0:T(8,128)(2,1)S(1)}, s16[16,9472]{1,0:T(8,128)(2,1)S(1)}, u32[]{:S(2)}, u32[]{:S(2)}) collective-permute-start(s16[16,9472]{1,0:T(8,128)(2,1)S(1)} %get-tuple-element.35), channel_id=1, source_target_pairs={{0,8},{8,0},{4,12},{12,4},{16,24},{24,16},{20,28},{28,20},{1,9},{9... | collective-permute-start | bytes 909320 | tf_op jit(solution)/shard_map/ppermute | solution.py:507
  12.4 21.7 %copy-start.15 = (s32[32]{0:T(128)S(1)}, s32[32]{0:T(128)}, u32[]{:S(2)}) copy-start(s32[32]{0:T(128)} %cut_ref.5) | copy-start | bytes 388
  12.4 21.7 %copy-start.1 = (bf16[4,1536,256]{2,1,0:T(8,128)(2,1)S(1)}, bf16[4,1536,256]{2,1,0:T(8,128)(2,1)}, u32[]{:S(2)}) copy-start(bf16[4,1536,256]{2,1,0:T(8,128)(2,1)} %constant.53.clone.table_ref) | copy-start | bytes 9437188
  12.4 10.0 %collective-permute-start.3 = (s16[16,9472]{1,0:T(8,128)(2,1)S(1)}, s16[16,9472]{1,0:T(8,128)(2,1)S(1)}, u32[]{:S(2)}, u32[]{:S(2)}) collective-permute-start(s16[16,9472]{1,0:T(8,128)(2,1)S(1)} %get-tuple-element.34), channel_id=1, source_target_pairs={{8,16},{16,8},{12,20},{20,12},{9,17},{17,9},{13,21},{21,13},{10,18... | collective-permute-start | bytes 909320 | tf_op jit(solution)/shard_map/ppermute | solution.py:508
  21.7 0.8 %copy-start.11 = (s16[16,15616]{1,0:T(8,128)(2,1)}, s16[16,15616]{1,0:T(8,128)(2,1)S(1)}, u32[]{:S(2)}) copy-start(s16[16,15616]{1,0:T(8,128)(2,1)S(1)} %collective-permute-done.1.inner_ref) | copy-start | bytes 1499140
  22.4 1.4 %copy-start.4 = (f32[2,4,16,3072]{3,2,1,0:T(8,128)S(1)}, f32[2,4,16,3072]{3,2,1,0:T(8,128)}, u32[]{:S(2)}) copy-start(f32[2,4,16,3072]{3,2,1,0:T(8,128)} %fields_ref.5) | copy-start | bytes 4718596
  23.9 1.1 %copy-start.6 = (bf16[2,4,16,3072]{3,2,1,0:T(8,128)(2,1)S(1)}, bf16[2,4,16,3072]{3,2,1,0:T(8,128)(2,1)}, u32[]{:S(2)}) copy-start(bf16[2,4,16,3072]{3,2,1,0:T(8,128)(2,1)} %courant_ref.5) | copy-start | bytes 2359300
  25.0 1.0 %copy-start.12 = (s16[16,15616]{1,0:T(8,128)(2,1)S(1)}, s16[16,15616]{1,0:T(8,128)(2,1)}, u32[]{:S(2)}) copy-start(s16[16,15616]{1,0:T(8,128)(2,1)} %copy-done.11) | copy-start | bytes 1499140
  30.8 5.5 %collective-permute-start.4 = (s16[16,6400]{1,0:T(8,128)(2,1)S(1)}, s16[16,6400]{1,0:T(8,128)(2,1)S(1)}, u32[]{:S(2)}, u32[]{:S(2)}) collective-permute-start(s16[16,6400]{1,0:T(8,128)(2,1)S(1)} %get-tuple-element.24), channel_id=1, source_target_pairs={{0,8},{8,0},{4,12},{12,4},{16,24},{24,16},{20,28},{28,20},{1,9},{9... | collective-permute-start | bytes 614408 | tf_op jit(solution)/shard_map/ppermute | solution.py:528
  32.2 6.5 %collective-permute-start.5 = (s16[16,6400]{1,0:T(8,128)(2,1)S(1)}, s16[16,6400]{1,0:T(8,128)(2,1)S(1)}, u32[]{:S(2)}, u32[]{:S(2)}) collective-permute-start(s16[16,6400]{1,0:T(8,128)(2,1)S(1)} %get-tuple-element.25), channel_id=1, source_target_pairs={{8,16},{16,8},{12,20},{20,12},{9,17},{17,9},{13,21},{21,13},{10,18... | collective-permute-start | bytes 614408 | tf_op jit(solution)/shard_map/ppermute | solution.py:529
  36.2 4.3 %copy-start.7 = (f32[8,2,8,3328]{3,2,1,0:T(8,128)}, f32[8,2,8,3328]{3,2,1,0:T(8,128)S(1)}, u32[]{:S(2)}) copy-start(f32[8,2,8,3328]{3,2,1,0:T(8,128)S(1)} %get-tuple-element.22.new_ref) | copy-start | bytes 5111812
  36.3 4.3 %copy-start.9 = (f32[4,2,8,3072]{3,2,1,0:T(8,128)}, f32[4,2,8,3072]{3,2,1,0:T(8,128)S(1)}, u32[]{:S(2)}) copy-start(f32[4,2,8,3072]{3,2,1,0:T(8,128)S(1)} %get-tuple-element.23.inner_ref) | copy-start | bytes 2359300
  40.6 13.9 %collective-permute-start.10 = (s16[16,3200]{1,0:T(8,128)(2,1)S(1)}, s16[16,3200]{1,0:T(8,128)(2,1)S(1)}, u32[]{:S(2)}, u32[]{:S(2)}) collective-permute-start(s16[16,3200]{1,0:T(8,128)(2,1)S(1)} %get-tuple-element.31), channel_id=1, source_target_pairs={{0,5},{1,4},{2,7},{3,6},{4,1},{5,0},{6,3},{7,2},{8,13},{9,12},{10,... | collective-permute-start | bytes 307208 | tf_op jit(solution)/shard_map/ppermute | solution.py:566
  44.7 11.0 %collective-permute-start.11 = (s16[16,3200]{1,0:T(8,128)(2,1)S(1)}, s16[16,3200]{1,0:T(8,128)(2,1)S(1)}, u32[]{:S(2)}, u32[]{:S(2)}) collective-permute-start(s16[16,3200]{1,0:T(8,128)(2,1)S(1)} %get-tuple-element.32), channel_id=1, source_target_pairs={{0,6},{1,7},{2,4},{3,5},{4,2},{5,3},{6,0},{7,1},{8,14},{9,15},{10,... | collective-permute-start | bytes 307208 | tf_op jit(solution)/shard_map/ppermute | solution.py:566
  45.9 10.3 %collective-permute-start.12 = (s16[16,3200]{1,0:T(8,128)(2,1)S(1)}, s16[16,3200]{1,0:T(8,128)(2,1)S(1)}, u32[]{:S(2)}, u32[]{:S(2)}) collective-permute-start(s16[16,3200]{1,0:T(8,128)(2,1)S(1)} %get-tuple-element.33), channel_id=1, source_target_pairs={{0,7},{1,6},{2,5},{3,4},{4,3},{5,2},{6,1},{7,0},{8,15},{9,14},{10,... | collective-permute-start | bytes 307208 | tf_op jit(solution)/shard_map/ppermute | solution.py:566
  46.2 10.0 %collective-permute-start.9 = (s16[16,3200]{1,0:T(8,128)(2,1)S(1)}, s16[16,3200]{1,0:T(8,128)(2,1)S(1)}, u32[]{:S(2)}, u32[]{:S(2)}) collective-permute-start(s16[16,3200]{1,0:T(8,128)(2,1)S(1)} %get-tuple-element.26.refs_0_), channel_id=1, source_target_pairs={{0,4},{1,5},{2,6},{3,7},{4,0},{5,1},{6,2},{7,3},{8,12},{9,13},{10,... | collective-permute-start | bytes 307208 | tf_op jit(solution)/shard_map/ppermute | solution.py:566
  47.4 1.9 %copy-start.2 = (bf16[4,1536,256]{2,1,0:T(8,128)(2,1)S(1)}, bf16[4,1536,256]{2,1,0:T(8,128)(2,1)}, u32[]{:S(2)}) copy-start(bf16[4,1536,256]{2,1,0:T(8,128)(2,1)} %constant.53.clone.table_ref) | copy-start | bytes 9437188
  49.3 1.5 %copy-start.8 = (f32[8,2,8,3328]{3,2,1,0:T(8,128)S(1)}, f32[8,2,8,3328]{3,2,1,0:T(8,128)}, u32[]{:S(2)}) copy-start(f32[8,2,8,3328]{3,2,1,0:T(8,128)} %copy-done.7) | copy-start | bytes 5111812
  50.8 1.1 %copy-start.10 = (f32[4,2,8,3072]{3,2,1,0:T(8,128)S(1)}, f32[4,2,8,3072]{3,2,1,0:T(8,128)}, u32[]{:S(2)}) copy-start(f32[4,2,8,3072]{3,2,1,0:T(8,128)} %copy-done.9) | copy-start | bytes 2359300
  51.9 9.3 %copy-start.13 = (f32[64,192]{1,0:T(8,128)S(1)}, f32[64,192]{1,0:T(8,128)}, u32[]{:S(2)}) copy-start(f32[64,192]{1,0:T(8,128)} %constant.54.clone.refs_10_) | copy-start | bytes 147460
  51.9 9.3 %copy-start.14 = (f32[64,64]{1,0:T(8,128)S(1)}, f32[64,64]{1,0:T(8,128)}, u32[]{:S(2)}) copy-start(f32[64,64]{1,0:T(8,128)} %refs_9_.1) | copy-start | bytes 49156
  53.8 2.4 %collective-permute-start.6 = (s16[16,3200]{1,0:T(8,128)(2,1)S(1)}, s16[16,3200]{1,0:T(8,128)(2,1)S(1)}, u32[]{:S(2)}, u32[]{:S(2)}) collective-permute-start(s16[16,3200]{1,0:T(8,128)(2,1)S(1)} %get-tuple-element.28), channel_id=1, source_target_pairs={{0,1},{1,0},{2,3},{3,2},{4,5},{5,4},{6,7},{7,6},{8,9},{9,8},{10,11... | collective-permute-start | bytes 307208 | tf_op jit(solution)/shard_map/ppermute | solution.py:578
  54.4 4.5 %collective-permute-start.7 = (s16[16,3200]{1,0:T(8,128)(2,1)S(1)}, s16[16,3200]{1,0:T(8,128)(2,1)S(1)}, u32[]{:S(2)}, u32[]{:S(2)}) collective-permute-start(s16[16,3200]{1,0:T(8,128)(2,1)S(1)} %get-tuple-element.29), channel_id=1, source_target_pairs={{0,2},{1,3},{2,0},{3,1},{4,6},{5,7},{6,4},{7,5},{8,10},{9,11},{10,... | collective-permute-start | bytes 307208 | tf_op jit(solution)/shard_map/ppermute | solution.py:578
  55.7 5.6 %collective-permute-start.8 = (s16[16,3200]{1,0:T(8,128)(2,1)S(1)}, s16[16,3200]{1,0:T(8,128)(2,1)S(1)}, u32[]{:S(2)}, u32[]{:S(2)}) collective-permute-start(s16[16,3200]{1,0:T(8,128)(2,1)S(1)} %get-tuple-element.30), channel_id=1, source_target_pairs={{0,3},{1,2},{2,1},{3,0},{4,7},{5,6},{6,5},{7,4},{8,11},{9,10},{10,... | collective-permute-start | bytes 307208 | tf_op jit(solution)/shard_map/ppermute | solution.py:578
where the time goes:
time: 64.9 us; the launch traced here: 64.4 us
  starting transfers between devices  17.6 us (27%)
  waiting for transfers between devices  17.6 us (27%)
  Pallas kernels  16.7 us (26%)
  local copies, waits for them, and re-layouts  11.4 us (18%)
  between operations  0.82 us (1%)
    unnamed x32, local copies, waits for them, and re-layouts  11.4 us
    ppermute x1, waiting for transfers between devices, shards(): inner = lax.ppermute(inner, 'lat', swap)  7.06 us
    ppermute x4, starting transfers between devices, shards(): got.append(lax.ppermute(block, ('lat', 'lev'), pairs))  6.86 us
    ppermute x3, waiting for transfers between devices, shards(): got.insert(b, lax.ppermute(block, 'lev', pairs) if b else block)  5.02 us
    pallas_call x1, Pallas kernels, shards(): pl.pallas_call(functools.partial(first_kernel, z), name='first', in_specs...  4.77 us
    pallas_call x2, Pallas kernels, outer(): pl.pallas_call(functools.partial(outer_kernel, z, parts, partner), name='...  3.74 us
    pallas_call x1, Pallas kernels, shards(): pl.pallas_call(functools.partial(column_kernel, z, parts), name='columns'...  3.15 us
    ppermute x1, waiting for transfers between devices, shards(): edge = lax.ppermute(edge, 'lat', swap)  3.14 us
  transfers between devices with their start and end apart: 13, of which 5 were waited for; matrix products, arithmetic and copies ran while one was open for 0% of the time, Pallas kernels for 8%

commit v1 on v0

--- a/solution.py
+++ b/solution.py
@@ -17,7 +17,7 @@
 TINY = 2.0**-100
 WIND = 81920.0
 ROUND = 1.5 * 2.0**23
-VMEM_LIMIT = 12 * 2**20
+VMEM_LIMIT = 7 * 2**20
 VMEM_MOST = 63 * 2**20 + 2**19
 
 

time: 64.9 us -> 64.8 us (level)
  no operation moved by 1% of the time
where the time goes in v1:
time: 64.8 us; the launch traced here: 64.4 us
  starting transfers between devices  17.6 us (27%)
  waiting for transfers between devices  17.6 us (27%)
  Pallas kernels  16.7 us (26%)
  local copies, waits for them, and re-layouts  11.4 us (18%)
  between operations  0.82 us (1%)
    unnamed x32, local copies, waits for them, and re-layouts  11.4 us
    ppermute x1, waiting for transfers between devices, shards(): inner = lax.ppermute(inner, 'lat', swap)  7.06 us
    ppermute x4, starting transfers between devices, shards(): got.append(lax.ppermute(block, ('lat', 'lev'), pairs))  6.86 us
    ppermute x3, waiting for transfers between devices, shards(): got.insert(b, lax.ppermute(block, 'lev', pairs) if b else block)  5.02 us
    pallas_call x1, Pallas kernels, shards(): pl.pallas_call(functools.partial(first_kernel, z), name='first', in_specs...  4.77 us
    pallas_call x2, Pallas kernels, outer(): pl.pallas_call(functools.partial(outer_kernel, z, parts, partner), name='...  3.74 us
    pallas_call x1, Pallas kernels, shards(): pl.pallas_call(functools.partial(column_kernel, z, parts), name='columns'...  3.15 us
    ppermute x1, waiting for transfers between devices, shards(): edge = lax.ppermute(edge, 'lat', swap)  3.14 us
  transfers between devices with their start and end apart: 13, of which 5 were waited for; matrix products, arithmetic and copies ran while one was open for 0% of the time, Pallas kernels for 8%

profile of v1, /device:TPU:17, one launch (start us, length us, event | category | flops | bytes accessed | tf_op | source)
XLA Modules:
  0.0 64.4 jit_solution(12442684184606533741)
XLA Ops:
  0.6 0.0 copy-start
  0.6 2.0 %edge.1 = s16[16,9472]{1,0:T(8,128)(2,1)} custom-call(f32[2,4,16,3072]{3,2,1,0:T(8,128)} %fields_ref.5, bf16[2,4,16,3072]{3,2,1,0:T(8,128)(2,1)} %courant_ref.5), custom_call_target="tpu_custom_call" | custom-call | flops 1000 | bytes 1000 | tf_op jit(solution)/shard_map/edge/pallas_call | solution.py:481
  2.6 1.3 %collective-permute-start = (s16[16,9472]{1,0:T(8,128)(2,1)}, s16[16,9472]{1,0:T(8,128)(2,1)S(1)}, u32[]{:S(2)}, u32[]{:S(2)}) collective-permute-start(s16[16,9472]{1,0:T(8,128)(2,1)} %edge.1), channel_id=1, source_target_pairs={{0,4},{4,0},{8,12},{12,8},{16,20},{20,16},{24,28},{28,24},{1,5},{5... | collective-permute-start | bytes 909320 | tf_op jit(solution)/shard_map/ppermute | solution.py:495
  3.9 0.1 pad_add_fusion.par_ref
  4.0 1.4 %copy-done.3 = f32[2,4,16,3072]{3,2,1,0:T(8,128)S(1)} copy-done((f32[2,4,16,3072]{3,2,1,0:T(8,128)S(1)}, f32[2,4,16,3072]{3,2,1,0:T(8,128)}, u32[]{:S(2)}) %copy-start.3) | copy-done | bytes 1572888
  5.4 1.1 %copy-done.5 = bf16[2,4,16,3072]{3,2,1,0:T(8,128)(2,1)S(1)} copy-done((bf16[2,4,16,3072]{3,2,1,0:T(8,128)(2,1)S(1)}, bf16[2,4,16,3072]{3,2,1,0:T(8,128)(2,1)}, u32[]{:S(2)}) %copy-start.5) | copy-done | bytes 786456
  6.5 1.0 %rest.1 = (s16[16,15616]{1,0:T(8,128)(2,1)S(1)}, s16[16,9472]{1,0:T(8,128)(2,1)S(1)}) custom-call(s32[4]{0:T(128)S(1)} %pad_add_fusion.par_ref, f32[2,4,16,3072]{3,2,1,0:T(8,128)S(1)} %copy-done.3, bf16[2,4,16,3072]{3,2,1,0:T(8,128)(2,1)S(1)} %copy-done.5), custom_call_target="tpu_custom_call" | custom-call | flops 1000 | bytes 1000 | tf_op jit(solution)/shard_map/rest/pallas_call | solution.py:496
  7.5 0.3 collective-permute-start.1
  7.8 3.1 %collective-permute-done.edge_ref = s16[16,9472]{1,0:T(8,128)(2,1)S(1)} collective-permute-done((s16[16,9472]{1,0:T(8,128)(2,1)}, s16[16,9472]{1,0:T(8,128)(2,1)S(1)}, u32[]{:S(2)}, u32[]{:S(2)}) %collective-permute-start) | collective-permute-done | bytes 303136 | tf_op jit(solution)/shard_map/ppermute | solution.py:495
  11.0 0.1 broadcast_select_fusion
  11.1 1.4 %collective-permute-start.2 = (s16[16,9472]{1,0:T(8,128)(2,1)S(1)}, s16[16,9472]{1,0:T(8,128)(2,1)S(1)}, u32[]{:S(2)}, u32[]{:S(2)}) collective-permute-start(s16[16,9472]{1,0:T(8,128)(2,1)S(1)} %get-tuple-element.35), channel_id=1, source_target_pairs={{0,8},{8,0},{4,12},{12,4},{16,24},{24,16},{20,28},{28,20},{1,9},{9... | collective-permute-start | bytes 909320 | tf_op jit(solution)/shard_map/ppermute | solution.py:507
  12.4 2.2 %collective-permute-start.3 = (s16[16,9472]{1,0:T(8,128)(2,1)S(1)}, s16[16,9472]{1,0:T(8,128)(2,1)S(1)}, u32[]{:S(2)}, u32[]{:S(2)}) collective-permute-start(s16[16,9472]{1,0:T(8,128)(2,1)S(1)} %get-tuple-element.34), channel_id=1, source_target_pairs={{8,16},{16,8},{12,20},{20,12},{9,17},{17,9},{13,21},{21,13},{10,18... | collective-permute-start | bytes 909320 | tf_op jit(solution)/shard_map/ppermute | solution.py:508
  14.6 7.1 %collective-permute-done.1.inner_ref = s16[16,15616]{1,0:T(8,128)(2,1)S(1)} collective-permute-done((s16[16,15616]{1,0:T(8,128)(2,1)S(1)}, s16[16,15616]{1,0:T(8,128)(2,1)S(1)}, u32[]{:S(2)}, u32[]{:S(2)}) %collective-permute-start.1) | collective-permute-done | bytes 499744 | tf_op jit(solution)/shard_map/ppermute | solution.py:505
  21.7 0.8 %copy-done.11 = s16[16,15616]{1,0:T(8,128)(2,1)} copy-done((s16[16,15616]{1,0:T(8,128)(2,1)}, s16[16,15616]{1,0:T(8,128)(2,1)S(1)}, u32[]{:S(2)}) %copy-start.11) | copy-done | bytes 499736
  22.4 0.0 collective-permute-done.2.one_ref
  22.4 0.0 collective-permute-done.3.two_ref
  22.5 1.4 %copy-done.4 = f32[2,4,16,3072]{3,2,1,0:T(8,128)S(1)} copy-done((f32[2,4,16,3072]{3,2,1,0:T(8,128)S(1)}, f32[2,4,16,3072]{3,2,1,0:T(8,128)}, u32[]{:S(2)}) %copy-start.4) | copy-done | bytes 1572888
  23.9 1.1 %copy-done.6 = bf16[2,4,16,3072]{3,2,1,0:T(8,128)(2,1)S(1)} copy-done((bf16[2,4,16,3072]{3,2,1,0:T(8,128)(2,1)S(1)}, bf16[2,4,16,3072]{3,2,1,0:T(8,128)(2,1)}, u32[]{:S(2)}) %copy-start.6) | copy-done | bytes 786456
  25.0 1.0 %copy-done.12 = s16[16,15616]{1,0:T(8,128)(2,1)S(1)} copy-done((s16[16,15616]{1,0:T(8,128)(2,1)S(1)}, s16[16,15616]{1,0:T(8,128)(2,1)}, u32[]{:S(2)}) %copy-start.12) | copy-done | bytes 499736
  26.0 4.8 %first.1 = (f32[8,2,8,3328]{3,2,1,0:T(8,128)S(1)}, f32[25,8,3072]{2,1,0:T(8,128)S(1)}, s16[16,6400]{1,0:T(8,128)(2,1)S(1)}, s16[16,6400]{1,0:T(8,128)(2,1)S(1)}) custom-call(s32[4]{0:T(128)S(1)} %pad_add_fusion.par_ref, f32[2,4,16,3072]{3,2,1,0:T(8,128)S(1)} %copy-done.4, bf16[2,4,16,3072]{3,2,1,0:T(8,128)(2,1)S(1)} %copy-done.6, ...), custom_call_target="tpu_custom_call" | custom-call | flops 1000 | bytes 1000 | tf_op jit(solution)/shard_map/first/pallas_call | solution.py:509
  30.8 1.4 %collective-permute-start.4 = (s16[16,6400]{1,0:T(8,128)(2,1)S(1)}, s16[16,6400]{1,0:T(8,128)(2,1)S(1)}, u32[]{:S(2)}, u32[]{:S(2)}) collective-permute-start(s16[16,6400]{1,0:T(8,128)(2,1)S(1)} %get-tuple-element.24), channel_id=1, source_target_pairs={{0,8},{8,0},{4,12},{12,4},{16,24},{24,16},{20,28},{28,20},{1,9},{9... | collective-permute-start | bytes 614408 | tf_op jit(solution)/shard_map/ppermute | solution.py:528
  32.2 1.9 %collective-permute-start.5 = (s16[16,6400]{1,0:T(8,128)(2,1)S(1)}, s16[16,6400]{1,0:T(8,128)(2,1)S(1)}, u32[]{:S(2)}, u32[]{:S(2)}) collective-permute-start(s16[16,6400]{1,0:T(8,128)(2,1)S(1)} %get-tuple-element.25), channel_id=1, source_target_pairs={{8,16},{16,8},{12,20},{20,12},{9,17},{17,9},{13,21},{21,13},{10,18... | collective-permute-start | bytes 614408 | tf_op jit(solution)/shard_map/ppermute | solution.py:529
  34.1 2.1 %inner.1 = (f32[8,2,8,3328]{3,2,1,0:T(8,128)S(1)}, f32[4,2,8,3072]{3,2,1,0:T(8,128)S(1)}) custom-call(s32[4]{0:T(128)S(1)} %pad_add_fusion.par_ref, s32[32]{0:T(128)S(1)} %copy-done.15, f32[8,2,8,3328]{3,2,1,0:T(8,128)S(1)} %get-tuple-element.20.in_ref, f32[25,8,3072]{2,1,0:T(8,128)S(1)} %get-tuple-element.21.winds_ref, bf16[4,1536,256]{2,1,0:T(8,128)(2,1)S(1)} %copy-done.1), custom_call_target="tpu_custom_call" | custom-call | flops 1000 | bytes 1000 | tf_op jit(solution)/shard_map/inner/pallas_call | solution.py:532
  36.2 0.0 copy-start.7
  36.3 0.0 copy-start.9
  36.3 0.0 collective-permute-done.4.one_ref
  36.3 2.4 %collective-permute-done.5.two_ref = s16[16,6400]{1,0:T(8,128)(2,1)S(1)} collective-permute-done((s16[16,6400]{1,0:T(8,128)(2,1)S(1)}, s16[16,6400]{1,0:T(8,128)(2,1)S(1)}, u32[]{:S(2)}, u32[]{:S(2)}) %collective-permute-start.5) | collective-permute-done | bytes 204832 | tf_op jit(solution)/shard_map/ppermute | solution.py:529
  38.7 1.9 %outer_partner.1 = (s16[16,3200]{1,0:T(8,128)(2,1)S(1)}, s16[16,3200]{1,0:T(8,128)(2,1)S(1)}, s16[16,3200]{1,0:T(8,128)(2,1)S(1)}, s16[16,3200]{1,0:T(8,128)(2,1)S(1)}) custom-call(s32[4]{0:T(128)S(1)} %pad_add_fusion.par_ref, s32[32]{0:T(128)S(1)} %copy-done.15, f32[8,2,8,3328]{3,2,1,0:T(8,128)S(1)} %get-tuple-element.22.new_ref, ...), custom_call_target="tpu_custom_call" | custom-call | flops 1000 | bytes 1000 | tf_op jit(solution)/shard_map/outer_partner/pallas_call | solution.py:546
  40.6 4.1 %collective-permute-start.10 = (s16[16,3200]{1,0:T(8,128)(2,1)S(1)}, s16[16,3200]{1,0:T(8,128)(2,1)S(1)}, u32[]{:S(2)}, u32[]{:S(2)}) collective-permute-start(s16[16,3200]{1,0:T(8,128)(2,1)S(1)} %get-tuple-element.31), channel_id=1, source_target_pairs={{0,5},{1,4},{2,7},{3,6},{4,1},{5,0},{6,3},{7,2},{8,13},{9,12},{10,... | collective-permute-start | bytes 307208 | tf_op jit(solution)/shard_map/ppermute | solution.py:566
  44.7 1.2 %collective-permute-start.11 = (s16[16,3200]{1,0:T(8,128)(2,1)S(1)}, s16[16,3200]{1,0:T(8,128)(2,1)S(1)}, u32[]{:S(2)}, u32[]{:S(2)}) collective-permute-start(s16[16,3200]{1,0:T(8,128)(2,1)S(1)} %get-tuple-element.32), channel_id=1, source_target_pairs={{0,6},{1,7},{2,4},{3,5},{4,2},{5,3},{6,0},{7,1},{8,14},{9,15},{10,... | collective-permute-start | bytes 307208 | tf_op jit(solution)/shard_map/ppermute | solution.py:566
  45.9 0.3 collective-permute-start.12
  46.2 1.2 %collective-permute-start.9 = (s16[16,3200]{1,0:T(8,128)(2,1)S(1)}, s16[16,3200]{1,0:T(8,128)(2,1)S(1)}, u32[]{:S(2)}, u32[]{:S(2)}) collective-permute-start(s16[16,3200]{1,0:T(8,128)(2,1)S(1)} %get-tuple-element.26.refs_0_), channel_id=1, source_target_pairs={{0,4},{1,5},{2,6},{3,7},{4,0},{5,1},{6,2},{7,3},{8,12},{9,13},{10,... | collective-permute-start | bytes 307208 | tf_op jit(solution)/shard_map/ppermute | solution.py:566
  47.4 1.9 %copy-done.2 = bf16[4,1536,256]{2,1,0:T(8,128)(2,1)S(1)} copy-done((bf16[4,1536,256]{2,1,0:T(8,128)(2,1)S(1)}, bf16[4,1536,256]{2,1,0:T(8,128)(2,1)}, u32[]{:S(2)}) %copy-start.2) | copy-done | bytes 3145752
  49.3 1.5 %copy-done.8 = f32[8,2,8,3328]{3,2,1,0:T(8,128)S(1)} copy-done((f32[8,2,8,3328]{3,2,1,0:T(8,128)S(1)}, f32[8,2,8,3328]{3,2,1,0:T(8,128)}, u32[]{:S(2)}) %copy-start.8) | copy-done | bytes 1703960
  50.8 1.1 %copy-done.10 = f32[4,2,8,3072]{3,2,1,0:T(8,128)S(1)} copy-done((f32[4,2,8,3072]{3,2,1,0:T(8,128)S(1)}, f32[4,2,8,3072]{3,2,1,0:T(8,128)}, u32[]{:S(2)}) %copy-start.10) | copy-done | bytes 786456
  51.9 1.9 %outer_own.1 = (s16[16,3200]{1,0:T(8,128)(2,1)S(1)}, s16[16,3200]{1,0:T(8,128)(2,1)S(1)}, s16[16,3200]{1,0:T(8,128)(2,1)S(1)}, s16[16,3200]{1,0:T(8,128)(2,1)S(1)}) custom-call(s32[4]{0:T(128)S(1)} %pad_add_fusion.par_ref, s32[32]{0:T(128)S(1)} %copy-done.15, f32[8,2,8,3328]{3,2,1,0:T(8,128)S(1)} %copy-done.8, f32[4,2,8,3072]{3,2,1,0:T(8,128)S(1)} %copy-done.10, ...), custom_call_target="tpu_custom_call" | custom-call | flops 1000 | bytes 1000 | tf_op jit(solution)/shard_map/outer_own/pallas_call | solution.py:546
  53.8 0.6 collective-permute-start.6
  54.4 0.0 collective-permute-done.10.refs_1_.refs_5_
  54.4 1.3 %collective-permute-start.7 = (s16[16,3200]{1,0:T(8,128)(2,1)S(1)}, s16[16,3200]{1,0:T(8,128)(2,1)S(1)}, u32[]{:S(2)}, u32[]{:S(2)}) collective-permute-start(s16[16,3200]{1,0:T(8,128)(2,1)S(1)} %get-tuple-element.29), channel_id=1, source_target_pairs={{0,2},{1,3},{2,0},{3,1},{4,6},{5,7},{6,4},{7,5},{8,10},{9,11},{10,... | collective-permute-start | bytes 307208 | tf_op jit(solution)/shard_map/ppermute | solution.py:578
  55.7 0.0 collective-permute-done.11.refs_2_.refs_6_
  55.7 0.5 collective-permute-start.8
  56.2 0.0 collective-permute-done.12.refs_3_.refs_7_
  56.2 0.0 collective-permute-done.9.refs_0_.refs_4_
  56.2 0.0 collective-permute-done.6.refs_1_
  56.2 2.7 %collective-permute-done.7.refs_2_ = s16[16,3200]{1,0:T(8,128)(2,1)S(1)} collective-permute-done((s16[16,3200]{1,0:T(8,128)(2,1)S(1)}, s16[16,3200]{1,0:T(8,128)(2,1)S(1)}, u32[]{:S(2)}, u32[]{:S(2)}) %collective-permute-start.7) | collective-permute-done | bytes 102432 | tf_op jit(solution)/shard_map/ppermute | solution.py:578
  58.9 2.4 %collective-permute-done.8.refs_3_ = s16[16,3200]{1,0:T(8,128)(2,1)S(1)} collective-permute-done((s16[16,3200]{1,0:T(8,128)(2,1)S(1)}, s16[16,3200]{1,0:T(8,128)(2,1)S(1)}, u32[]{:S(2)}, u32[]{:S(2)}) %collective-permute-start.8) | collective-permute-done | bytes 102432 | tf_op jit(solution)/shard_map/ppermute | solution.py:578
  61.2 0.0 copy-done.14
  61.2 3.2 %columns.1 = (f32[2,4,64,768]{3,2,1,0:T(8,128)}, f32[4,64,768]{2,1,0:T(8,128)}) custom-call(s32[4]{0:T(128)S(1)} %pad_add_fusion.par_ref, s16[16,3200]{1,0:T(8,128)(2,1)S(1)} %get-tuple-element.27.refs_0_, s16[16,3200]{1,0:T(8,128)(2,1)S(1)} %collective-permute-done.6.refs_1_, s16[16,3200]{1,0:T(8,128)(2,1)S(1)} %collective-permute-done.7.refs_2_, ...), custom_call_target="tpu_custom_call" | custom-call | flops 1000 | bytes 1000 | tf_op jit(solution)/shard_map/columns/pallas_call | solution.py:584
  (22 shorter events, 0.1 us)
Async XLA Ops:
  0.6 55.5 %copy-start = (f32[4,3072]{1,0:T(4,128)S(1)}, f32[4,3072]{1,0:T(4,128)}, u32[]{:S(2)}) copy-start(f32[4,3072]{1,0:T(4,128)} %param.10) | copy-start | bytes 147460
  2.6 8.3 %collective-permute-start = (s16[16,9472]{1,0:T(8,128)(2,1)}, s16[16,9472]{1,0:T(8,128)(2,1)S(1)}, u32[]{:S(2)}, u32[]{:S(2)}) collective-permute-start(s16[16,9472]{1,0:T(8,128)(2,1)} %edge.1), channel_id=1, source_target_pairs={{0,4},{4,0},{8,12},{12,8},{16,20},{20,16},{24,28},{28,24},{1,5},{5... | collective-permute-start | bytes 909320 | tf_op jit(solution)/shard_map/ppermute | solution.py:495
  4.0 1.4 %copy-start.3 = (f32[2,4,16,3072]{3,2,1,0:T(8,128)S(1)}, f32[2,4,16,3072]{3,2,1,0:T(8,128)}, u32[]{:S(2)}) copy-start(f32[2,4,16,3072]{3,2,1,0:T(8,128)} %fields_ref.5) | copy-start | bytes 4718596
  5.4 1.1 %copy-start.5 = (bf16[2,4,16,3072]{3,2,1,0:T(8,128)(2,1)S(1)}, bf16[2,4,16,3072]{3,2,1,0:T(8,128)(2,1)}, u32[]{:S(2)}) copy-start(bf16[2,4,16,3072]{3,2,1,0:T(8,128)(2,1)} %courant_ref.5) | copy-start | bytes 2359300
  7.5 14.2 %collective-permute-start.1 = (s16[16,15616]{1,0:T(8,128)(2,1)S(1)}, s16[16,15616]{1,0:T(8,128)(2,1)S(1)}, u32[]{:S(2)}, u32[]{:S(2)}) collective-permute-start(s16[16,15616]{1,0:T(8,128)(2,1)S(1)} %get-tuple-element.18), channel_id=1, source_target_pairs={{0,4},{4,0},{8,12},{12,8},{16,20},{20,16},{24,28},{28,24},{1,5},{5... | collective-permute-start | bytes 1499144 | tf_op jit(solution)/shard_map/ppermute | solution.py:505
  11.1 11.4 %collective-permute-start.2 = (s16[16,9472]{1,0:T(8,128)(2,1)S(1)}, s16[16,9472]{1,0:T(8,128)(2,1)S(1)}, u32[]{:S(2)}, u32[]{:S(2)}) collective-permute-start(s16[16,9472]{1,0:T(8,128)(2,1)S(1)} %get-tuple-element.35), channel_id=1, source_target_pairs={{0,8},{8,0},{4,12},{12,4},{16,24},{24,16},{20,28},{28,20},{1,9},{9... | collective-permute-start | bytes 909320 | tf_op jit(solution)/shard_map/ppermute | solution.py:507
  12.4 21.7 %copy-start.15 = (s32[32]{0:T(128)S(1)}, s32[32]{0:T(128)}, u32[]{:S(2)}) copy-start(s32[32]{0:T(128)} %cut_ref.5) | copy-start | bytes 388
  12.4 21.7 %copy-start.1 = (bf16[4,1536,256]{2,1,0:T(8,128)(2,1)S(1)}, bf16[4,1536,256]{2,1,0:T(8,128)(2,1)}, u32[]{:S(2)}) copy-start(bf16[4,1536,256]{2,1,0:T(8,128)(2,1)} %constant.53.clone.table_ref) | copy-start | bytes 9437188
  12.4 10.0 %collective-permute-start.3 = (s16[16,9472]{1,0:T(8,128)(2,1)S(1)}, s16[16,9472]{1,0:T(8,128)(2,1)S(1)}, u32[]{:S(2)}, u32[]{:S(2)}) collective-permute-start(s16[16,9472]{1,0:T(8,128)(2,1)S(1)} %get-tuple-element.34), channel_id=1, source_target_pairs={{8,16},{16,8},{12,20},{20,12},{9,17},{17,9},{13,21},{21,13},{10,18... | collective-permute-start | bytes 909320 | tf_op jit(solution)/shard_map/ppermute | solution.py:508
  21.7 0.8 %copy-start.11 = (s16[16,15616]{1,0:T(8,128)(2,1)}, s16[16,15616]{1,0:T(8,128)(2,1)S(1)}, u32[]{:S(2)}) copy-start(s16[16,15616]{1,0:T(8,128)(2,1)S(1)} %collective-permute-done.1.inner_ref) | copy-start | bytes 1499140
  22.4 1.4 %copy-start.4 = (f32[2,4,16,3072]{3,2,1,0:T(8,128)S(1)}, f32[2,4,16,3072]{3,2,1,0:T(8,128)}, u32[]{:S(2)}) copy-start(f32[2,4,16,3072]{3,2,1,0:T(8,128)} %fields_ref.5) | copy-start | bytes 4718596
  23.9 1.1 %copy-start.6 = (bf16[2,4,16,3072]{3,2,1,0:T(8,128)(2,1)S(1)}, bf16[2,4,16,3072]{3,2,1,0:T(8,128)(2,1)}, u32[]{:S(2)}) copy-start(bf16[2,4,16,3072]{3,2,1,0:T(8,128)(2,1)} %courant_ref.5) | copy-start | bytes 2359300
  25.0 1.0 %copy-start.12 = (s16[16,15616]{1,0:T(8,128)(2,1)S(1)}, s16[16,15616]{1,0:T(8,128)(2,1)}, u32[]{:S(2)}) copy-start(s16[16,15616]{1,0:T(8,128)(2,1)} %copy-done.11) | copy-start | bytes 1499140
  30.8 5.5 %collective-permute-start.4 = (s16[16,6400]{1,0:T(8,128)(2,1)S(1)}, s16[16,6400]{1,0:T(8,128)(2,1)S(1)}, u32[]{:S(2)}, u32[]{:S(2)}) collective-permute-start(s16[16,6400]{1,0:T(8,128)(2,1)S(1)} %get-tuple-element.24), channel_id=1, source_target_pairs={{0,8},{8,0},{4,12},{12,4},{16,24},{24,16},{20,28},{28,20},{1,9},{9... | collective-permute-start | bytes 614408 | tf_op jit(solution)/shard_map/ppermute | solution.py:528
  32.2 6.5 %collective-permute-start.5 = (s16[16,6400]{1,0:T(8,128)(2,1)S(1)}, s16[16,6400]{1,0:T(8,128)(2,1)S(1)}, u32[]{:S(2)}, u32[]{:S(2)}) collective-permute-start(s16[16,6400]{1,0:T(8,128)(2,1)S(1)} %get-tuple-element.25), channel_id=1, source_target_pairs={{8,16},{16,8},{12,20},{20,12},{9,17},{17,9},{13,21},{21,13},{10,18... | collective-permute-start | bytes 614408 | tf_op jit(solution)/shard_map/ppermute | solution.py:529
  36.2 4.3 %copy-start.7 = (f32[8,2,8,3328]{3,2,1,0:T(8,128)}, f32[8,2,8,3328]{3,2,1,0:T(8,128)S(1)}, u32[]{:S(2)}) copy-start(f32[8,2,8,3328]{3,2,1,0:T(8,128)S(1)} %get-tuple-element.22.new_ref) | copy-start | bytes 5111812
  36.3 4.3 %copy-start.9 = (f32[4,2,8,3072]{3,2,1,0:T(8,128)}, f32[4,2,8,3072]{3,2,1,0:T(8,128)S(1)}, u32[]{:S(2)}) copy-start(f32[4,2,8,3072]{3,2,1,0:T(8,128)S(1)} %get-tuple-element.23.inner_ref) | copy-start | bytes 2359300
  40.6 13.9 %collective-permute-start.10 = (s16[16,3200]{1,0:T(8,128)(2,1)S(1)}, s16[16,3200]{1,0:T(8,128)(2,1)S(1)}, u32[]{:S(2)}, u32[]{:S(2)}) collective-permute-start(s16[16,3200]{1,0:T(8,128)(2,1)S(1)} %get-tuple-element.31), channel_id=1, source_target_pairs={{0,5},{1,4},{2,7},{3,6},{4,1},{5,0},{6,3},{7,2},{8,13},{9,12},{10,... | collective-permute-start | bytes 307208 | tf_op jit(solution)/shard_map/ppermute | solution.py:566
  44.7 11.0 %collective-permute-start.11 = (s16[16,3200]{1,0:T(8,128)(2,1)S(1)}, s16[16,3200]{1,0:T(8,128)(2,1)S(1)}, u32[]{:S(2)}, u32[]{:S(2)}) collective-permute-start(s16[16,3200]{1,0:T(8,128)(2,1)S(1)} %get-tuple-element.32), channel_id=1, source_target_pairs={{0,6},{1,7},{2,4},{3,5},{4,2},{5,3},{6,0},{7,1},{8,14},{9,15},{10,... | collective-permute-start | bytes 307208 | tf_op jit(solution)/shard_map/ppermute | solution.py:566
  45.9 10.3 %collective-permute-start.12 = (s16[16,3200]{1,0:T(8,128)(2,1)S(1)}, s16[16,3200]{1,0:T(8,128)(2,1)S(1)}, u32[]{:S(2)}, u32[]{:S(2)}) collective-permute-start(s16[16,3200]{1,0:T(8,128)(2,1)S(1)} %get-tuple-element.33), channel_id=1, source_target_pairs={{0,7},{1,6},{2,5},{3,4},{4,3},{5,2},{6,1},{7,0},{8,15},{9,14},{10,... | collective-permute-start | bytes 307208 | tf_op jit(solution)/shard_map/ppermute | solution.py:566
  46.2 10.0 %collective-permute-start.9 = (s16[16,3200]{1,0:T(8,128)(2,1)S(1)}, s16[16,3200]{1,0:T(8,128)(2,1)S(1)}, u32[]{:S(2)}, u32[]{:S(2)}) collective-permute-start(s16[16,3200]{1,0:T(8,128)(2,1)S(1)} %get-tuple-element.26.refs_0_), channel_id=1, source_target_pairs={{0,4},{1,5},{2,6},{3,7},{4,0},{5,1},{6,2},{7,3},{8,12},{9,13},{10,... | collective-permute-start | bytes 307208 | tf_op jit(solution)/shard_map/ppermute | solution.py:566
  47.4 1.9 %copy-start.2 = (bf16[4,1536,256]{2,1,0:T(8,128)(2,1)S(1)}, bf16[4,1536,256]{2,1,0:T(8,128)(2,1)}, u32[]{:S(2)}) copy-start(bf16[4,1536,256]{2,1,0:T(8,128)(2,1)} %constant.53.clone.table_ref) | copy-start | bytes 9437188
  49.3 1.5 %copy-start.8 = (f32[8,2,8,3328]{3,2,1,0:T(8,128)S(1)}, f32[8,2,8,3328]{3,2,1,0:T(8,128)}, u32[]{:S(2)}) copy-start(f32[8,2,8,3328]{3,2,1,0:T(8,128)} %copy-done.7) | copy-start | bytes 5111812
  50.8 1.1 %copy-start.10 = (f32[4,2,8,3072]{3,2,1,0:T(8,128)S(1)}, f32[4,2,8,3072]{3,2,1,0:T(8,128)}, u32[]{:S(2)}) copy-start(f32[4,2,8,3072]{3,2,1,0:T(8,128)} %copy-done.9) | copy-start | bytes 2359300
  51.9 9.3 %copy-start.13 = (f32[64,192]{1,0:T(8,128)S(1)}, f32[64,192]{1,0:T(8,128)}, u32[]{:S(2)}) copy-start(f32[64,192]{1,0:T(8,128)} %constant.54.clone.refs_10_) | copy-start | bytes 147460
  51.9 9.3 %copy-start.14 = (f32[64,64]{1,0:T(8,128)S(1)}, f32[64,64]{1,0:T(8,128)}, u32[]{:S(2)}) copy-start(f32[64,64]{1,0:T(8,128)} %refs_9_.1) | copy-start | bytes 49156
  53.8 2.4 %collective-permute-start.6 = (s16[16,3200]{1,0:T(8,128)(2,1)S(1)}, s16[16,3200]{1,0:T(8,128)(2,1)S(1)}, u32[]{:S(2)}, u32[]{:S(2)}) collective-permute-start(s16[16,3200]{1,0:T(8,128)(2,1)S(1)} %get-tuple-element.28), channel_id=1, source_target_pairs={{0,1},{1,0},{2,3},{3,2},{4,5},{5,4},{6,7},{7,6},{8,9},{9,8},{10,11... | collective-permute-start | bytes 307208 | tf_op jit(solution)/shard_map/ppermute | solution.py:578
  54.4 4.5 %collective-permute-start.7 = (s16[16,3200]{1,0:T(8,128)(2,1)S(1)}, s16[16,3200]{1,0:T(8,128)(2,1)S(1)}, u32[]{:S(2)}, u32[]{:S(2)}) collective-permute-start(s16[16,3200]{1,0:T(8,128)(2,1)S(1)} %get-tuple-element.29), channel_id=1, source_target_pairs={{0,2},{1,3},{2,0},{3,1},{4,6},{5,7},{6,4},{7,5},{8,10},{9,11},{10,... | collective-permute-start | bytes 307208 | tf_op jit(solution)/shard_map/ppermute | solution.py:578
  55.7 5.6 %collective-permute-start.8 = (s16[16,3200]{1,0:T(8,128)(2,1)S(1)}, s16[16,3200]{1,0:T(8,128)(2,1)S(1)}, u32[]{:S(2)}, u32[]{:S(2)}) collective-permute-start(s16[16,3200]{1,0:T(8,128)(2,1)S(1)} %get-tuple-element.30), channel_id=1, source_target_pairs={{0,3},{1,2},{2,1},{3,0},{4,7},{5,6},{6,5},{7,4},{8,11},{9,10},{10,... | collective-permute-start | bytes 307208 | tf_op jit(solution)/shard_map/ppermute | solution.py:578

commit v2 on v0

--- a/solution.py
+++ b/solution.py
@@ -75,7 +75,6 @@
         self.pad = lon + 2 * LANE
         self.code = lon + LANE
         self.edge = 2 * self.code + lon
-        self.inner = 2 * self.code + 3 * lon
 
 
 def put_padded(ref, index, values, lon):
@@ -119,7 +118,7 @@
     edge_ref[:, 2 * z.code :] = wind_row(z, wind_ref, 1 - p)
 
 
-def rest_kernel(z, par_ref, fields_ref, courant_ref, inner_ref, own_ref):
+def rest_kernel(z, par_ref, fields_ref, courant_ref, middle_ref, last_ref, own_ref):
     p = par_ref[0]
     keep = pl.multiple_of(p * z.half, z.half)
     give = pl.multiple_of((1 - p) * z.half, z.half)
@@ -133,12 +132,22 @@
     edge, inner = 2 * p, 2 * (1 - p)
     at = 2 * z.code
     for r in range(2):
-        encode_row(field_row(inner + r, give), inner_ref, r * z.code)
-    for i, row in enumerate((inner, inner + 1, 1 + p)):
-        inner_ref[:, at + i * z.lon : at + (i + 1) * z.lon] = winds(row, 1 - p)
-    for r in range(2):
+        encode_row(field_row(inner + r, give), middle_ref, r * z.code)
         encode_row(field_row(edge + r, keep), own_ref, r * z.code)
+        last_ref[:, r * z.lon : (r + 1) * z.lon] = winds(1 + r, 1 - p)
+    middle_ref[:, at : at + z.lon] = winds(3 * (1 - p), 1 - p)
     own_ref[:, at : at + z.lon] = winds(3 * p, p)
+
+
+def pick_kernel(par_ref, own_ref, edge_ref, one_ref, two_ref):
+    straight = par_ref[0] + par_ref[3] == 1
+
+    def put(a_ref, b_ref):
+        one_ref[...] = a_ref[...]
+        two_ref[...] = b_ref[...]
+
+    pl.when(straight)(lambda: put(own_ref, edge_ref))
+    pl.when(jnp.logical_not(straight))(lambda: put(edge_ref, own_ref))
 
 
 def shifted(pieces, shift, lanes):
@@ -173,7 +182,7 @@
                 east = 7.0 * (u[k] + p1) - (m1 + p2)
                 west = 7.0 * (m1 + u[k]) - (m2 + p1)
                 east = winds_ref[base + j, :, piece(k)] * east
-                out.append(east - winds_ref[z.band + base + j, :, piece(k)] * west)
+                out.append(east - winds_ref[z.rows + base + j, :, piece(k)] * west)
             return out
 
         for f in range(2):
@@ -184,7 +193,7 @@
             for j in range(count_rows + 1):
                 later = start(j, f) if 0 < j < count_rows else None
                 new = [
-                    winds_ref[2 * z.band + base + j, :, piece(k)] * (8.0 * sums[1][k] - (sums[0][k] + sums[2][k]))
+                    winds_ref[2 * z.rows + base + j, :, piece(k)] * (8.0 * sums[1][k] - (sums[0][k] + sums[2][k]))
                     for k in range(count)
                 ]
                 if j > 0:
@@ -273,77 +282,141 @@
                 store(start + r, smooth[r])
 
 
-def first_kernel(
-    z, par_ref, fields_ref, courant_ref, edge_ref, inner_ref, one_ref, two_ref,
-    new_ref, winds_ref, one_out_ref, two_out_ref, u_ref, cx_ref, cy_ref,
+def received_winds(z, in_ref, at):
+    values = in_ref[:, at : at + z.lon].astype(jnp.int32).astype(jnp.float32) * (1.0 / WIND)
+    return values[: z.half], values[z.half :]
+
+
+def own_winds(z, p, courant_ref, row):
+    got = []
+    for k in range(2):
+        wind = courant_ref[k, row].astype(jnp.float32)
+        got.append(jnp.where(p == 1, wind[z.half :], wind[: z.half]))
+    return got
+
+
+def faces(z, cx_ref, cy_ref, winds_ref):
+    def face_rows(j, carry):
+        wind = cx_ref[j] * (1.0 / 24.0)
+        here = wind[:, LANE : LANE + z.lon]
+        winds_ref[j] = here + pltpu.roll(wind, z.pad - 1, 1)[:, LANE : LANE + z.lon]
+        winds_ref[z.rows + j] = here + pltpu.roll(wind, 1, 1)[:, LANE : LANE + z.lon]
+        return carry
+
+    lax.fori_loop(0, z.rows, face_rows, 0)
+    for j in range(z.rows + 1):
+        winds_ref[2 * z.rows + j] = (cy_ref[j] + cy_ref[j + 1]) * (1.0 / 24.0)
+
+
+def writer(new_ref):
+    def write(row, f, at, k, values):
+        new_ref[row, f, :, pl.ds(pl.multiple_of(at + (k + 1) * LANE, LANE), LANE)] = values
+
+    return write
+
+
+def wrap(z, new_ref, rows):
+    for j in rows:
+        new_ref[j, :, :, 0:LANE] = new_ref[j, :, :, z.lon : z.lon + LANE]
+        new_ref[j, :, :, LANE + z.lon :] = new_ref[j, :, :, LANE : 2 * LANE]
+
+
+def encode_new(z, new_ref, row, out_ref):
+    for r in range(2):
+        values = new_ref[row + r, :, :, LANE : LANE + z.lon]
+        encode_row(values.reshape(2 * z.half, z.lon), out_ref, r * z.code)
+
+
+def own_kernel(
+    z, par_ref, fields_ref, courant_ref, edge_ref, middle_ref, one_ref, two_ref,
+    new_ref, winds_ref, code_ref, u_ref, cx_ref, cy_ref,
 ):
     p, b = par_ref[0], par_ref[3]
     lon, half = z.lon, z.half
 
-    def pair(values):
-        return values.reshape(2, half, values.shape[1])
-
-    def winds(in_ref, at):
-        values = in_ref[:, at : at + lon].astype(jnp.int32).astype(jnp.float32) * (1.0 / WIND)
-        return values[:half], values[half:]
-
-    def place_wind(row, east, north):
-        put_padded(cx_ref, (row,), east, lon)
-        cy_ref[row + 1] = north
+    def place(row, in_ref, r):
+        values = decode_row(in_ref, r * z.code, lon)
+        put_padded(u_ref, (row + r,), values.reshape(2, half, lon), lon)
 
     keep = pl.multiple_of(p * half, half)
     for r in range(z.rows):
-        row = z.rows * p + r
         own = jnp.stack([fields_ref[f, r, pl.ds(keep, half)] for f in range(2)])
-        put_padded(u_ref, (row + 2,), own, lon)
-        got = []
-        for k in range(2):
-            wind = courant_ref[k, r].astype(jnp.float32)
-            got.append(jnp.where(p == 1, wind[half:], wind[:half]))
-        place_wind(row, *got)
+        put_padded(u_ref, (z.rows * p + r + 2,), own, lon)
+        east, north = own_winds(z, p, courant_ref, r)
+        put_padded(cx_ref, (r,), east, lon)
+        cy_ref[r + 1] = north
+    for r in range(2):
+        place(6 * (1 - p) + 2, edge_ref, r)
+        place(4 - 2 * p + 2, middle_ref, r)
+        place(10 * (1 - b), one_ref, r)
+        place(10 * b, two_ref, r)
     at = 2 * z.code
-    for r in range(2):
-        put_padded(u_ref, (6 * (1 - p) + r + 2,), pair(decode_row(edge_ref, r * z.code, lon)), lon)
-        put_padded(u_ref, (4 - 2 * p + r + 2,), pair(decode_row(inner_ref, r * z.code, lon)), lon)
-        put_padded(u_ref, (10 * (1 - b) + r,), pair(decode_row(one_ref, r * z.code, lon)), lon)
-        put_padded(u_ref, (10 * b + r,), pair(decode_row(two_ref, r * z.code, lon)), lon)
-        place_wind(4 - 2 * p + r, *winds(inner_ref, at + r * lon))
-    place_wind(7 * (1 - p), *winds(edge_ref, at))
-    place_wind(6 - 5 * p, *winds(inner_ref, at + 2 * lon))
-    cy_ref[9 * (1 - b)] = winds(one_ref, at)[1]
-    cy_ref[9 * b] = winds(two_ref, at)[1]
-
-    def face_rows(j, carry):
-        wind = cx_ref[j] * (1.0 / 24.0)
-        here = wind[:, LANE : LANE + lon]
-        winds_ref[j] = here + pltpu.roll(wind, z.pad - 1, 1)[:, LANE : LANE + lon]
-        winds_ref[z.band + j] = here + pltpu.roll(wind, 1, 1)[:, LANE : LANE + lon]
-        return carry
-
-    lax.fori_loop(0, z.band, face_rows, 0)
-
-    def face_cols(j, carry):
-        winds_ref[2 * z.band + j] = (cy_ref[j] + cy_ref[j + 1]) * (1.0 / 24.0)
-        return carry
-
-    lax.fori_loop(0, z.band + 1, face_cols, 0)
+    cy_ref[5 * (1 - p)] = received_winds(z, middle_ref, at)[1]
+
+    def halo(in_ref):
+        cy_ref[5 * p] = received_winds(z, in_ref, at)[1]
+
+    pl.when(p + b == 1)(lambda: halo(one_ref))
+    pl.when(p + b != 1)(lambda: halo(two_ref))
+    faces(z, cx_ref, cy_ref, winds_ref)
+    start = z.rows * p
+    substep(z, z.rows, 0, lambda j, f, piece: u_ref[start + j, f, :, piece], winds_ref, writer(new_ref))
+    encode_new(z, new_ref, 2 * p, code_ref)
+    wrap(z, new_ref, range(z.rows))
+
+
+def other_kernel(
+    z, par_ref, courant_ref, edge_ref, middle_ref, last_ref, one_ref, two_ref, u_ref, own_code_ref,
+    new_ref, winds_ref, one_out_ref, two_out_ref, cx_ref, cy_ref,
+):
+    p, b = par_ref[0], par_ref[3]
+    at = 2 * z.code
+
+    def place(row, winds):
+        put_padded(cx_ref, (row,), winds[0], z.lon)
+        cy_ref[row + 1] = winds[1]
+
+    place(3 * (1 - p), received_winds(z, edge_ref, at))
+    place(3 * p, received_winds(z, middle_ref, at))
+    place(1, received_winds(z, last_ref, 0))
+    place(2, received_winds(z, last_ref, z.lon))
+    cy_ref[5 * p] = own_winds(z, p, courant_ref, 3 * (1 - p))[1]
+
+    def halo(in_ref):
+        cy_ref[5 * (1 - p)] = received_winds(z, in_ref, at)[1]
+
+    pl.when(p + b == 1)(lambda: halo(two_ref))
+    pl.when(p + b != 1)(lambda: halo(one_ref))
+    faces(z, cx_ref, cy_ref, winds_ref)
+    outer = 2 * (1 - p)
+    start = z.rows * (1 - p) + outer
+    substep(z, 2, outer, lambda j, f, piece: u_ref[start + j, f, :, piece], winds_ref, writer(new_ref))
+
+    def codes(mine_ref, other_ref):
+        mine_ref[...] = own_code_ref[...]
+        encode_new(z, new_ref, 0, other_ref)
+
+    pl.when(p + b == 1)(lambda: codes(one_out_ref, two_out_ref))
+    pl.when(p + b != 1)(lambda: codes(two_out_ref, one_out_ref))
+    wrap(z, new_ref, range(2))
+
+
+def inner_kernel(
+    z, par_ref, cut_ref, own_ref, other_ref, u_ref, own_winds_ref, other_winds_ref, table_ref, new_ref, inner_ref
+):
+    p = par_ref[0]
+    own, other = z.rows * p, z.rows * (1 - p)
+    for j in range(z.rows):
+        new_ref[own + j] = own_ref[j]
+    for j in range(2):
+        new_ref[other + 2 * (1 - p) + j] = other_ref[j]
+    start = other + 2 * p
 
     def write(row, f, at, k, values):
-        new_ref[row, f, :, pl.ds(pl.multiple_of(at + (k + 1) * LANE, LANE), LANE)] = values
-
-    substep(z, z.band, 0, lambda j, f, piece: u_ref[j, f, :, piece], winds_ref, write)
-    for r in range(2):
-        for row, out_ref in ((6 * (1 - b) + r, one_out_ref), (6 * b + r, two_out_ref)):
-            values = new_ref[row, :, :, LANE : LANE + lon]
-            encode_row(values.reshape(2 * half, lon), out_ref, r * z.code)
-    for j in range(z.band):
-        new_ref[j, :, :, 0:LANE] = new_ref[j, :, :, lon : lon + LANE]
-        new_ref[j, :, :, LANE + lon :] = new_ref[j, :, :, LANE : 2 * LANE]
-
-
-def inner_kernel(z, par_ref, cut_ref, in_ref, winds_ref, table_ref, new_ref, inner_ref):
-    for j in range(z.band):
-        new_ref[j] = in_ref[j]
+        writer(new_ref)(start + row, f, at, k, values)
+
+    substep(z, 2, 2 * p, lambda j, f, piece: u_ref[start + j, f, :, piece], other_winds_ref, write)
+    wrap(z, new_ref, (start, start + 1))
 
     def store(row, values):
         put_padded(new_ref, (row,), values, z.lon)
@@ -351,23 +424,39 @@
     for part in range(2):
         filter_rows(
             z, cut_ref, par_ref[1], part * z.rows, table_ref,
-            lambda row: in_ref[row, :, :, LANE : LANE + z.lon], store,
+            lambda row: new_ref[row, :, :, LANE : LANE + z.lon], store,
         )
-
-    def write(row, f, at, k, values):
-        inner_ref[row, f, :, pl.ds(pl.multiple_of(at + k * LANE, LANE), LANE)] = values
-
-    substep(z, z.band - 4, 2, lambda j, f, piece: new_ref[j, f, :, piece], winds_ref, write)
+    for i, (low, base, winds_ref) in enumerate(
+        ((2 * p, 2 * (1 - p), own_winds_ref), (2 * (1 - p), 2 * p, other_winds_ref))
+    ):
+
+        def keep(row, f, at, k, values):
+            inner_ref[2 * i + row, f, :, pl.ds(pl.multiple_of(at + k * LANE, LANE), LANE)] = values
+
+        substep(z, 2, base, lambda j, f, piece: new_ref[low + j, f, :, piece], winds_ref, keep)
 
 
 def outer_kernel(
-    z, parts, partner, par_ref, cut_ref, new_ref, inner_ref, winds_ref, one_ref, two_ref, table_ref, *refs
+    z, parts, par_ref, cut_ref, new_ref, inner_ref, own_winds_ref, other_winds_ref, one_ref, two_ref, table_ref, *refs
 ):
-    refs = refs if partner else refs[1:]
-    out_refs, (u_ref, v_ref) = refs[:parts], refs[parts:]
+    out_refs, (u_ref, v_ref) = refs[: 2 * parts], refs[2 * parts :]
+    p = par_ref[0]
+    outer_half(
+        z, parts, 1 - p, 2, par_ref, cut_ref, new_ref, inner_ref, other_winds_ref, one_ref, two_ref, table_ref,
+        out_refs[:parts], u_ref, v_ref,
+    )
+    outer_half(
+        z, parts, p, 0, par_ref, cut_ref, new_ref, inner_ref, own_winds_ref, one_ref, two_ref, table_ref,
+        out_refs[parts:], u_ref, v_ref,
+    )
+
+
+def outer_half(
+    z, parts, side, inner_at, par_ref, cut_ref, new_ref, inner_ref, winds_ref, one_ref, two_ref, table_ref,
+    out_refs, u_ref, v_ref,
+):
     lon, half = z.lon, z.half
     tall = 2 * half
-    side = 1 - par_ref[0] if partner else par_ref[0]
     base = z.rows * side
 
     def halo(in_ref):
@@ -381,12 +470,12 @@
     for r in range(4):
         u_ref[2 * (1 - side) + r] = new_ref[base + r]
     for r in range(2):
-        v_ref[2 * (1 - side) + r] = inner_ref[2 * side + r]
+        v_ref[2 * (1 - side) + r] = inner_ref[inner_at + r]
 
     def write(row, f, at, k, values):
         v_ref[2 * side + row, f, :, pl.ds(pl.multiple_of(at + k * LANE, LANE), LANE)] = values
 
-    substep(z, 2, 6 * side, lambda j, f, piece: u_ref[j, f, :, piece], winds_ref, write)
+    substep(z, 2, 2 * side, lambda j, f, piece: u_ref[j, f, :, piece], winds_ref, write)
 
     def store(row, values):
         v_ref[row] = values
@@ -493,38 +582,63 @@
         cost_estimate=cost(),
     )(fields, courant)
     edge = lax.ppermute(edge, "lat", swap)
-    inner, own = pl.pallas_call(
+    middle, last, own = pl.pallas_call(
         functools.partial(rest_kernel, z),
         name="rest",
         in_specs=[scalars(), whole(), whole()],
+        out_specs=[whole()] * 3,
+        out_shape=[codes(tall, z.edge), codes(tall, 2 * lon), codes(tall, z.edge)],
+        compiler_params=params(),
+        cost_estimate=cost(),
+    )(place, fields, courant)
+    middle = lax.ppermute(middle, "lat", swap)
+    last = lax.ppermute(last, "lat", swap)
+    one, two = pl.pallas_call(
+        pick_kernel,
+        name="pick",
+        in_specs=[scalars(), whole(), whole()],
         out_specs=[whole()] * 2,
-        out_shape=[codes(tall, z.inner), codes(tall, z.edge)],
+        out_shape=[codes(tall, z.edge)] * 2,
         compiler_params=params(),
         cost_estimate=cost(),
-    )(place, fields, courant)
-    inner = lax.ppermute(inner, "lat", swap)
-    straight = (parity + (me // 2) % 2) == 1
-    one = lax.ppermute(jnp.where(straight, own, edge), "lat", ones)
-    two = lax.ppermute(jnp.where(straight, edge, own), "lat", twos)
-    new, winds, one_code, two_code = pl.pallas_call(
-        functools.partial(first_kernel, z),
-        name="first",
+    )(place, own, edge)
+    one = lax.ppermute(one, "lat", ones)
+    two = lax.ppermute(two, "lat", twos)
+
+    half_scratch = [
+        pltpu.VMEM((z.rows, z.half, z.pad), f32),
+        pltpu.VMEM((z.rows + 2, z.half, lon), f32),
+    ]
+    mine, own_winds, own_code, u = pl.pallas_call(
+        functools.partial(own_kernel, z),
+        name="own",
         in_specs=[scalars()] + [whole()] * 6,
         out_specs=[whole()] * 4,
         out_shape=[
-            shape(z.band, 2, z.half, z.pad),
-            shape(3 * z.band + 1, z.half, lon),
+            shape(z.rows, 2, z.half, z.pad),
+            shape(3 * z.rows + 1, z.half, lon),
+            codes(tall, 2 * z.code),
+            shape(z.band + 4, 2, z.half, z.pad),
+        ],
+        scratch_shapes=half_scratch,
+        compiler_params=params(),
+        cost_estimate=cost(),
+    )(place, fields, courant, edge, middle, one, two)
+    other, other_winds, one_code, two_code = pl.pallas_call(
+        functools.partial(other_kernel, z),
+        name="other",
+        in_specs=[scalars()] + [whole()] * 8,
+        out_specs=[whole()] * 4,
+        out_shape=[
+            shape(2, 2, z.half, z.pad),
+            shape(3 * z.rows + 1, z.half, lon),
             codes(tall, 2 * z.code),
             codes(tall, 2 * z.code),
         ],
-        scratch_shapes=[
-            pltpu.VMEM((z.band + 4, 2, z.half, z.pad), f32),
-            pltpu.VMEM((z.band, z.half, z.pad), f32),
-            pltpu.VMEM((z.band + 2, z.half, z.lon), f32),
-        ],
+        scratch_shapes=half_scratch,
         compiler_params=params(),
         cost_estimate=cost(),
-    )(place, fields, courant, edge, inner, one, two)
+    )(place, courant, edge, middle, last, one, two, u, own_code)
     one = lax.ppermute(one_code, "lat", ones)
     two = lax.ppermute(two_code, "lat", twos)
 
@@ -532,34 +646,29 @@
     new, inner = pl.pallas_call(
         functools.partial(inner_kernel, z),
         name="inner",
-        in_specs=[scalars(), scalars()] + [whole()] * 3,
+        in_specs=[scalars(), scalars()] + [whole()] * 6,
         out_specs=[whole()] * 2,
-        out_shape=[shape(z.band, 2, z.half, z.pad), shape(z.band - 4, 2, z.half, lon)],
+        out_shape=[shape(z.band, 2, z.half, z.pad), shape(z.rows, 2, z.half, lon)],
         compiler_params=params(),
         cost_estimate=cost(),
-    )(place, cutoffs, new, winds, tables)
+    )(place, cutoffs, mine, other, u, own_winds, other_winds, tables)
 
     column = lon // parts
-
-    def outer(*after):
-        partner = not after
-        return pl.pallas_call(
-            functools.partial(outer_kernel, z, parts, partner),
-            name="outer_partner" if partner else "outer_own",
-            in_specs=[scalars(), scalars()] + [whole()] * 6 + [far_memory()] * len(after),
-            out_specs=[whole()] * parts,
-            out_shape=[codes(tall, rows * column + LANE)] * parts,
-            scratch_shapes=[
-                pltpu.VMEM((6, 2, z.half, z.pad), f32),
-                pltpu.VMEM((z.rows, 2, z.half, lon), f32),
-            ],
-            compiler_params=params(),
-            cost_estimate=cost(),
-        )(place, cutoffs, new, inner, winds, one, two, tables, *after)
-
-    blocks = outer()
+    blocks = pl.pallas_call(
+        functools.partial(outer_kernel, z, parts),
+        name="outer",
+        in_specs=[scalars(), scalars()] + [whole()] * 7,
+        out_specs=[whole()] * (2 * parts),
+        out_shape=[codes(tall, rows * column + LANE)] * (2 * parts),
+        scratch_shapes=[
+            pltpu.VMEM((6, 2, z.half, z.pad), f32),
+            pltpu.VMEM((z.rows, 2, z.half, lon), f32),
+        ],
+        compiler_params=params(),
+        cost_estimate=cost(),
+    )(place, cutoffs, new, inner, own_winds, other_winds, one, two, tables)
     got = []
-    for b, block in enumerate(blocks):
+    for b, block in enumerate(blocks[:parts]):
         pairs = [
             (i * parts + j, (i ^ 1) * parts + (j ^ b)) for i in range(lats) for j in range(parts)
         ]
@@ -573,7 +682,7 @@
         compiler_params=params(),
         cost_estimate=cost(),
     )(*got)
-    for b, block in enumerate(outer(blocks[0])):
+    for b, block in enumerate(blocks[parts:]):
         pairs = [(j, j ^ b) for j in range(parts)]
         got.insert(b, lax.ppermute(block, "lev", pairs) if b else block)
 

time: 64.9 us -> 60.8 us (0.937)
  local copies, waits for them, and re-layouts: 11.4 us -> 2.6 us
  starting transfers between devices: 17.6 us -> 20.6 us
  Pallas kernels: 16.7 us -> 18.7 us
  waiting for transfers between devices: 17.6 us -> 16.9 us
    unnamed x32 -> x18, local copies, waits for them, and re-layouts: 11.4 us -> 2.58 us
    ppermute x4, waiting for transfers between devices: 0.01 us -> 4.27 us  [shards(): got.append(lax.ppermute(block, ('lat', 'lev'), pairs))]
    ppermute x3 -> x4, waiting for transfers between devices: 7.06 us -> 4.63 us  [the longest x1 3.15 us: shards(): two = lax.ppermute(two, 'lat', twos)]
    ppermute x4, starting transfers between devices: 6.86 us -> 9.08 us  [shards(): got.append(lax.ppermute(block, ('lat', 'lev'), pairs))]
    ppermute x1, waiting for transfers between devices: 2.38 us -> 0.94 us  [shards(): two = lax.ppermute(two_code, 'lat', twos)]
    pallas_call x1, Pallas kernels: 2.14 us -> 3.56 us  [shards(): pl.pallas_call(functools.partial(inner_kernel, z), name='inner', in_specs...]
    ppermute x1, starting transfers between devices: 1.36 us -> 0.07 us  [shards(): one = lax.ppermute(one_code, 'lat', ones)]
    ppermute x3, waiting for transfers between devices: 5.02 us -> 3.9 us  [shards(): got.insert(b, lax.ppermute(block, 'lev', pairs) if b else block)]
  transfers between devices with their start and end apart: 13 -> 14, of which waited for: 5 -> 10; matrix products, arithmetic and copies ran while one was open for 0% -> 0% of each run, Pallas kernels for 8% -> 14%
where the time goes in v2:
time: 60.8 us; the launch traced here: 59.7 us
  starting transfers between devices  20.6 us (34%)
  Pallas kernels  18.7 us (31%)
  waiting for transfers between devices  16.9 us (28%)
  local copies, waits for them, and re-layouts  2.6 us (4%)
  between operations  0.81 us (1%)
    ppermute x4, starting transfers between devices, shards(): got.append(lax.ppermute(block, ('lat', 'lev'), pairs))  9.08 us
    ppermute x4, waiting for transfers between devices, shards(): got.append(lax.ppermute(block, ('lat', 'lev'), pairs))  4.27 us
    ppermute x3, waiting for transfers between devices, shards(): got.insert(b, lax.ppermute(block, 'lev', pairs) if b else block)  3.9 us
    pallas_call x1, Pallas kernels, shards(): pl.pallas_call(functools.partial(inner_kernel, z), name='inner', in_specs...  3.56 us
    ppermute x3, starting transfers between devices, shards(): got.insert(b, lax.ppermute(block, 'lev', pairs) if b else block)  3.32 us
    pallas_call x1, Pallas kernels, shards(): pl.pallas_call(functools.partial(outer_kernel, z, parts), name='outer', i...  3.19 us
    pallas_call x1, Pallas kernels, shards(): pl.pallas_call(functools.partial(column_kernel, z, parts), name='columns'...  3.15 us
    ppermute x1, waiting for transfers between devices, shards(): two = lax.ppermute(two, 'lat', twos)  3.15 us
  transfers between devices with their start and end apart: 14, of which 10 were waited for; matrix products, arithmetic and copies ran while one was open for 0% of the time, Pallas kernels for 14%

profile of v2, /device:TPU:17, one launch (start us, length us, event | category | flops | bytes accessed | tf_op | source)
XLA Modules:
  0.0 59.7 jit_solution(5093485157245714084)
XLA Ops:
  0.6 0.0 copy-start
  0.6 2.0 %edge.1 = s16[16,9472]{1,0:T(8,128)(2,1)} custom-call(f32[2,4,16,3072]{3,2,1,0:T(8,128)} %fields_ref.5, bf16[2,4,16,3072]{3,2,1,0:T(8,128)(2,1)} %courant_ref.7), custom_call_target="tpu_custom_call" | custom-call | flops 1000 | bytes 1000 | tf_op jit(solution)/shard_map/edge/pallas_call | solution.py:570
  2.6 1.3 %collective-permute-start = (s16[16,9472]{1,0:T(8,128)(2,1)}, s16[16,9472]{1,0:T(8,128)(2,1)S(1)}, u32[]{:S(2)}, u32[]{:S(2)}) collective-permute-start(s16[16,9472]{1,0:T(8,128)(2,1)} %edge.1), channel_id=1, source_target_pairs={{0,4},{4,0},{8,12},{12,8},{16,20},{20,16},{24,28},{28,24},{1,5},{5... | collective-permute-start | bytes 909320 | tf_op jit(solution)/shard_map/ppermute | solution.py:584
  3.9 0.1 pad_add_fusion.par_ref
  4.0 1.4 %copy-done.1 = f32[2,4,16,3072]{3,2,1,0:T(8,128)S(1)} copy-done((f32[2,4,16,3072]{3,2,1,0:T(8,128)S(1)}, f32[2,4,16,3072]{3,2,1,0:T(8,128)}, u32[]{:S(2)}) %copy-start.1) | copy-done | bytes 1572888
  5.4 1.1 %copy-done.4 = bf16[2,4,16,3072]{3,2,1,0:T(8,128)(2,1)S(1)} copy-done((bf16[2,4,16,3072]{3,2,1,0:T(8,128)(2,1)S(1)}, bf16[2,4,16,3072]{3,2,1,0:T(8,128)(2,1)}, u32[]{:S(2)}) %copy-start.4) | copy-done | bytes 786456
  6.5 1.0 %rest.1 = (s16[16,9472]{1,0:T(8,128)(2,1)S(1)}, s16[16,6144]{1,0:T(8,128)(2,1)S(1)}, s16[16,9472]{1,0:T(8,128)(2,1)S(1)}) custom-call(s32[4]{0:T(128)S(1)} %pad_add_fusion.par_ref, f32[2,4,16,3072]{3,2,1,0:T(8,128)S(1)} %copy-done.1, bf16[2,4,16,3072]{3,2,1,0:T(8,128)(2,1)S(1)} %copy-done.4), custom_call_target="tpu_custom_call" | custom-call | flops 1000 | bytes 1000 | tf_op jit(solution)/shard_map/rest/pallas_call | solution.py:585
  7.5 0.3 collective-permute-start.1
  7.8 3.1 %collective-permute-done.edge_ref = s16[16,9472]{1,0:T(8,128)(2,1)S(1)} collective-permute-done((s16[16,9472]{1,0:T(8,128)(2,1)}, s16[16,9472]{1,0:T(8,128)(2,1)S(1)}, u32[]{:S(2)}, u32[]{:S(2)}) %collective-permute-start) | collective-permute-done | bytes 303136 | tf_op jit(solution)/shard_map/ppermute | solution.py:584
  11.0 0.6 pick.1
  11.5 1.4 %collective-permute-start.2 = (s16[16,9472]{1,0:T(8,128)(2,1)S(1)}, s16[16,9472]{1,0:T(8,128)(2,1)S(1)}, u32[]{:S(2)}, u32[]{:S(2)}) collective-permute-start(s16[16,9472]{1,0:T(8,128)(2,1)S(1)} %get-tuple-element.27), channel_id=1, source_target_pairs={{0,8},{8,0},{4,12},{12,4},{16,24},{24,16},{20,28},{28,20},{1,9},{9... | collective-permute-start | bytes 909320 | tf_op jit(solution)/shard_map/ppermute | solution.py:605
  12.9 1.9 %collective-permute-start.3 = (s16[16,9472]{1,0:T(8,128)(2,1)S(1)}, s16[16,9472]{1,0:T(8,128)(2,1)S(1)}, u32[]{:S(2)}, u32[]{:S(2)}) collective-permute-start(s16[16,9472]{1,0:T(8,128)(2,1)S(1)} %get-tuple-element.28), channel_id=1, source_target_pairs={{8,16},{16,8},{12,20},{20,12},{9,17},{17,9},{13,21},{21,13},{10,18... | collective-permute-start | bytes 909320 | tf_op jit(solution)/shard_map/ppermute | solution.py:606
  14.8 0.0 copy-start.5
  14.8 1.3 %collective-permute-start.4 = (s16[16,6144]{1,0:T(8,128)(2,1)S(1)}, s16[16,6144]{1,0:T(8,128)(2,1)S(1)}, u32[]{:S(2)}, u32[]{:S(2)}) collective-permute-start(s16[16,6144]{1,0:T(8,128)(2,1)S(1)} %get-tuple-element.30), channel_id=1, source_target_pairs={{0,4},{4,0},{8,12},{12,8},{16,20},{20,16},{24,28},{28,24},{1,5},{5... | collective-permute-start | bytes 589832 | tf_op jit(solution)/shard_map/ppermute | solution.py:595
  16.1 1.3 %collective-permute-done.1.middle_ref = s16[16,9472]{1,0:T(8,128)(2,1)S(1)} collective-permute-done((s16[16,9472]{1,0:T(8,128)(2,1)S(1)}, s16[16,9472]{1,0:T(8,128)(2,1)S(1)}, u32[]{:S(2)}, u32[]{:S(2)}) %collective-permute-start.1) | collective-permute-done | bytes 303136 | tf_op jit(solution)/shard_map/ppermute | solution.py:594
  17.4 0.1 collective-permute-done.2.one_ref
  17.6 3.2 %collective-permute-done.3.two_ref = s16[16,9472]{1,0:T(8,128)(2,1)S(1)} collective-permute-done((s16[16,9472]{1,0:T(8,128)(2,1)S(1)}, s16[16,9472]{1,0:T(8,128)(2,1)S(1)}, u32[]{:S(2)}, u32[]{:S(2)}) %collective-permute-start.3) | collective-permute-done | bytes 303136 | tf_op jit(solution)/shard_map/ppermute | solution.py:606
  20.7 0.0 copy-done.2
  20.8 3.0 %own.1 = (f32[4,2,8,3328]{3,2,1,0:T(8,128)S(1)}, f32[13,8,3072]{2,1,0:T(8,128)S(1)}, s16[16,6400]{1,0:T(8,128)(2,1)S(1)}, f32[12,2,8,3328]{3,2,1,0:T(8,128)S(1)}) custom-call(s32[4]{0:T(128)S(1)} %pad_add_fusion.par_ref, f32[2,4,16,3072]{3,2,1,0:T(8,128)S(1)} %copy-done.2, bf16[2,4,16,3072]{3,2,1,0:T(8,128)(2,1)S(1)} %copy-done.4, ...), custom_call_target="tpu_custom_call" | custom-call | flops 1000 | bytes 1000 | tf_op jit(solution)/shard_map/own/pallas_call | solution.py:612
  23.7 0.0 collective-permute-done.4.last_ref
  23.8 0.0 copy-done.5
  23.8 0.0 copy-start.3
  23.8 0.0 copy-start.8
  23.8 2.3 %other.1 = (f32[2,2,8,3328]{3,2,1,0:T(8,128)S(1)}, f32[13,8,3072]{2,1,0:T(8,128)S(1)}, s16[16,6400]{1,0:T(8,128)(2,1)S(1)}, s16[16,6400]{1,0:T(8,128)(2,1)S(1)}) custom-call(s32[4]{0:T(128)S(1)} %pad_add_fusion.par_ref, bf16[2,4,16,3072]{3,2,1,0:T(8,128)(2,1)S(1)} %copy-done.5, s16[16,9472]{1,0:T(8,128)(2,1)S(1)} %collective-permute-done.edge_ref, ...), custom_call_target="tpu_custom_call" | custom-call | flops 1000 | bytes 1000 | tf_op jit(solution)/shard_map/other/pallas_call | solution.py:627
  26.1 0.1 collective-permute-start.5
  26.2 2.0 %collective-permute-start.6 = (s16[16,6400]{1,0:T(8,128)(2,1)S(1)}, s16[16,6400]{1,0:T(8,128)(2,1)S(1)}, u32[]{:S(2)}, u32[]{:S(2)}) collective-permute-start(s16[16,6400]{1,0:T(8,128)(2,1)S(1)} %get-tuple-element.39), channel_id=1, source_target_pairs={{8,16},{16,8},{12,20},{20,12},{9,17},{17,9},{13,21},{21,13},{10,18... | collective-permute-start | bytes 614408 | tf_op jit(solution)/shard_map/ppermute | solution.py:643
  28.1 0.0 copy-done.3
  28.1 0.0 copy-done.8
  28.1 3.6 %inner.1 = (f32[8,2,8,3328]{3,2,1,0:T(8,128)S(1)}, f32[4,2,8,3072]{3,2,1,0:T(8,128)S(1)}) custom-call(s32[4]{0:T(128)S(1)} %pad_add_fusion.par_ref, s32[32]{0:T(128)S(1)} %copy-done.8, f32[4,2,8,3328]{3,2,1,0:T(8,128)S(1)} %get-tuple-element.29.own_ref, f32[2,2,8,3328]{3,2,1,0:T(8,128)S(1)} %get-tuple-element.33.other_ref, ...), custom_call_target="tpu_custom_call" | custom-call | flops 1000 | bytes 1000 | tf_op jit(solution)/shard_map/inner/pallas_call | solution.py:646
  31.7 0.0 collective-permute-done.5.one_ref
  31.7 0.9 %collective-permute-done.6.two_ref = s16[16,6400]{1,0:T(8,128)(2,1)S(1)} collective-permute-done((s16[16,6400]{1,0:T(8,128)(2,1)S(1)}, s16[16,6400]{1,0:T(8,128)(2,1)S(1)}, u32[]{:S(2)}, u32[]{:S(2)}) %collective-permute-start.6) | collective-permute-done | bytes 204832 | tf_op jit(solution)/shard_map/ppermute | solution.py:643
  32.7 3.2 %outer.1 = (s16[16,3200]{1,0:T(8,128)(2,1)S(1)}, s16[16,3200]{1,0:T(8,128)(2,1)S(1)}, s16[16,3200]{1,0:T(8,128)(2,1)S(1)}, s16[16,3200]{1,0:T(8,128)(2,1)S(1)}, ...) custom-call(s32[4]{0:T(128)S(1)} %pad_add_fusion.par_ref, ...), custom_call_target="tpu_custom_call" | custom-call | flops 1000 | bytes 1000 | tf_op jit(solution)/shard_map/outer/pallas_call | solution.py:657
  35.9 1.3 %collective-permute-start.10 = (s16[16,3200]{1,0:T(8,128)(2,1)S(1)}, s16[16,3200]{1,0:T(8,128)(2,1)S(1)}, u32[]{:S(2)}, u32[]{:S(2)}) collective-permute-start(s16[16,3200]{1,0:T(8,128)(2,1)S(1)} %get-tuple-element.44), channel_id=1, source_target_pairs={{0,4},{1,5},{2,6},{3,7},{4,0},{5,1},{6,2},{7,3},{8,12},{9,13},{10,... | collective-permute-start | bytes 307208 | tf_op jit(solution)/shard_map/ppermute | solution.py:675
  37.1 5.4 %collective-permute-start.11 = (s16[16,3200]{1,0:T(8,128)(2,1)S(1)}, s16[16,3200]{1,0:T(8,128)(2,1)S(1)}, u32[]{:S(2)}, u32[]{:S(2)}) collective-permute-start(s16[16,3200]{1,0:T(8,128)(2,1)S(1)} %get-tuple-element.45), channel_id=1, source_target_pairs={{0,5},{1,4},{2,7},{3,6},{4,1},{5,0},{6,3},{7,2},{8,13},{9,12},{10,... | collective-permute-start | bytes 307208 | tf_op jit(solution)/shard_map/ppermute | solution.py:675
  42.5 2.2 %collective-permute-start.12 = (s16[16,3200]{1,0:T(8,128)(2,1)S(1)}, s16[16,3200]{1,0:T(8,128)(2,1)S(1)}, u32[]{:S(2)}, u32[]{:S(2)}) collective-permute-start(s16[16,3200]{1,0:T(8,128)(2,1)S(1)} %get-tuple-element.46), channel_id=1, source_target_pairs={{0,6},{1,7},{2,4},{3,5},{4,2},{5,3},{6,0},{7,1},{8,14},{9,15},{10,... | collective-permute-start | bytes 307208 | tf_op jit(solution)/shard_map/ppermute | solution.py:675
  44.7 0.2 collective-permute-start.13
  45.0 0.3 collective-permute-start.7
  45.3 0.0 collective-permute-done.10.refs_0_.refs_4_
  45.3 1.2 %collective-permute-start.8 = (s16[16,3200]{1,0:T(8,128)(2,1)S(1)}, s16[16,3200]{1,0:T(8,128)(2,1)S(1)}, u32[]{:S(2)}, u32[]{:S(2)}) collective-permute-start(s16[16,3200]{1,0:T(8,128)(2,1)S(1)} %get-tuple-element.42), channel_id=1, source_target_pairs={{0,2},{1,3},{2,0},{3,1},{4,6},{5,7},{6,4},{7,5},{8,10},{9,11},{10,... | collective-permute-start | bytes 307208 | tf_op jit(solution)/shard_map/ppermute | solution.py:687
  46.5 0.7 %collective-permute-done.11.refs_1_.refs_5_ = s16[16,3200]{1,0:T(8,128)(2,1)S(1)} collective-permute-done((s16[16,3200]{1,0:T(8,128)(2,1)S(1)}, s16[16,3200]{1,0:T(8,128)(2,1)S(1)}, u32[]{:S(2)}, u32[]{:S(2)}) %collective-permute-start.11) | collective-permute-done | bytes 102432 | tf_op jit(solution)/shard_map/ppermute | solution.py:675
  47.3 1.7 %collective-permute-start.9 = (s16[16,3200]{1,0:T(8,128)(2,1)S(1)}, s16[16,3200]{1,0:T(8,128)(2,1)S(1)}, u32[]{:S(2)}, u32[]{:S(2)}) collective-permute-start(s16[16,3200]{1,0:T(8,128)(2,1)S(1)} %get-tuple-element.43), channel_id=1, source_target_pairs={{0,3},{1,2},{2,1},{3,0},{4,7},{5,6},{6,5},{7,4},{8,11},{9,10},{10,... | collective-permute-start | bytes 307208 | tf_op jit(solution)/shard_map/ppermute | solution.py:687
  49.0 1.4 %collective-permute-done.12.refs_2_.refs_6_ = s16[16,3200]{1,0:T(8,128)(2,1)S(1)} collective-permute-done((s16[16,3200]{1,0:T(8,128)(2,1)S(1)}, s16[16,3200]{1,0:T(8,128)(2,1)S(1)}, u32[]{:S(2)}, u32[]{:S(2)}) %collective-permute-start.12) | collective-permute-done | bytes 102432 | tf_op jit(solution)/shard_map/ppermute | solution.py:675
  50.4 2.2 %collective-permute-done.13.refs_3_.refs_7_ = s16[16,3200]{1,0:T(8,128)(2,1)S(1)} collective-permute-done((s16[16,3200]{1,0:T(8,128)(2,1)S(1)}, s16[16,3200]{1,0:T(8,128)(2,1)S(1)}, u32[]{:S(2)}, u32[]{:S(2)}) %collective-permute-start.13) | collective-permute-done | bytes 102432 | tf_op jit(solution)/shard_map/ppermute | solution.py:675
  52.6 0.0 collective-permute-done.7.refs_1_
  52.6 1.6 %collective-permute-done.8.refs_2_ = s16[16,3200]{1,0:T(8,128)(2,1)S(1)} collective-permute-done((s16[16,3200]{1,0:T(8,128)(2,1)S(1)}, s16[16,3200]{1,0:T(8,128)(2,1)S(1)}, u32[]{:S(2)}, u32[]{:S(2)}) %collective-permute-start.8) | collective-permute-done | bytes 102432 | tf_op jit(solution)/shard_map/ppermute | solution.py:687
  54.2 2.3 %collective-permute-done.9.refs_3_ = s16[16,3200]{1,0:T(8,128)(2,1)S(1)} collective-permute-done((s16[16,3200]{1,0:T(8,128)(2,1)S(1)}, s16[16,3200]{1,0:T(8,128)(2,1)S(1)}, u32[]{:S(2)}, u32[]{:S(2)}) %collective-permute-start.9) | collective-permute-done | bytes 102432 | tf_op jit(solution)/shard_map/ppermute | solution.py:687
  56.5 0.0 copy-done.6
  56.5 3.2 %columns.1 = (f32[2,4,64,768]{3,2,1,0:T(8,128)}, f32[4,64,768]{2,1,0:T(8,128)}) custom-call(s32[4]{0:T(128)S(1)} %pad_add_fusion.par_ref, s16[16,3200]{1,0:T(8,128)(2,1)S(1)} %get-tuple-element.40.refs_0_, s16[16,3200]{1,0:T(8,128)(2,1)S(1)} %collective-permute-done.7.refs_1_, s16[16,3200]{1,0:T(8,128)(2,1)S(1)} %collective-permute-done.8.refs_2_, ...), custom_call_target="tpu_custom_call" | custom-call | flops 1000 | bytes 1000 | tf_op jit(solution)/shard_map/columns/pallas_call | solution.py:693
  (10 shorter events, 0.0 us)
Async XLA Ops:
  0.6 48.4 %copy-start = (f32[4,3072]{1,0:T(4,128)S(1)}, f32[4,3072]{1,0:T(4,128)}, u32[]{:S(2)}) copy-start(f32[4,3072]{1,0:T(4,128)} %param.10) | copy-start | bytes 147460
  2.6 8.3 %collective-permute-start = (s16[16,9472]{1,0:T(8,128)(2,1)}, s16[16,9472]{1,0:T(8,128)(2,1)S(1)}, u32[]{:S(2)}, u32[]{:S(2)}) collective-permute-start(s16[16,9472]{1,0:T(8,128)(2,1)} %edge.1), channel_id=1, source_target_pairs={{0,4},{4,0},{8,12},{12,8},{16,20},{20,16},{24,28},{28,24},{1,5},{5... | collective-permute-start | bytes 909320 | tf_op jit(solution)/shard_map/ppermute | solution.py:584
  4.0 1.4 %copy-start.1 = (f32[2,4,16,3072]{3,2,1,0:T(8,128)S(1)}, f32[2,4,16,3072]{3,2,1,0:T(8,128)}, u32[]{:S(2)}) copy-start(f32[2,4,16,3072]{3,2,1,0:T(8,128)} %fields_ref.5) | copy-start | bytes 4718596
  5.4 1.1 %copy-start.4 = (bf16[2,4,16,3072]{3,2,1,0:T(8,128)(2,1)S(1)}, bf16[2,4,16,3072]{3,2,1,0:T(8,128)(2,1)}, u32[]{:S(2)}) copy-start(bf16[2,4,16,3072]{3,2,1,0:T(8,128)(2,1)} %courant_ref.7) | copy-start | bytes 2359300
  6.5 14.2 %copy-start.2 = (f32[2,4,16,3072]{3,2,1,0:T(8,128)S(1)}, f32[2,4,16,3072]{3,2,1,0:T(8,128)}, u32[]{:S(2)}) copy-start(f32[2,4,16,3072]{3,2,1,0:T(8,128)} %fields_ref.5) | copy-start | bytes 4718596
  7.5 10.0 %collective-permute-start.1 = (s16[16,9472]{1,0:T(8,128)(2,1)S(1)}, s16[16,9472]{1,0:T(8,128)(2,1)S(1)}, u32[]{:S(2)}, u32[]{:S(2)}) collective-permute-start(s16[16,9472]{1,0:T(8,128)(2,1)S(1)} %get-tuple-element.25), channel_id=1, source_target_pairs={{0,4},{4,0},{8,12},{12,8},{16,20},{20,16},{24,28},{28,24},{1,5},{5... | collective-permute-start | bytes 909320 | tf_op jit(solution)/shard_map/ppermute | solution.py:594
  11.5 6.0 %collective-permute-start.2 = (s16[16,9472]{1,0:T(8,128)(2,1)S(1)}, s16[16,9472]{1,0:T(8,128)(2,1)S(1)}, u32[]{:S(2)}, u32[]{:S(2)}) collective-permute-start(s16[16,9472]{1,0:T(8,128)(2,1)S(1)} %get-tuple-element.27), channel_id=1, source_target_pairs={{0,8},{8,0},{4,12},{12,4},{16,24},{24,16},{20,28},{28,20},{1,9},{9... | collective-permute-start | bytes 909320 | tf_op jit(solution)/shard_map/ppermute | solution.py:605
  12.9 7.8 %collective-permute-start.3 = (s16[16,9472]{1,0:T(8,128)(2,1)S(1)}, s16[16,9472]{1,0:T(8,128)(2,1)S(1)}, u32[]{:S(2)}, u32[]{:S(2)}) collective-permute-start(s16[16,9472]{1,0:T(8,128)(2,1)S(1)} %get-tuple-element.28), channel_id=1, source_target_pairs={{8,16},{16,8},{12,20},{20,12},{9,17},{17,9},{13,21},{21,13},{10,18... | collective-permute-start | bytes 909320 | tf_op jit(solution)/shard_map/ppermute | solution.py:606
  14.8 8.9 %copy-start.5 = (bf16[2,4,16,3072]{3,2,1,0:T(8,128)(2,1)S(1)}, bf16[2,4,16,3072]{3,2,1,0:T(8,128)(2,1)}, u32[]{:S(2)}) copy-start(bf16[2,4,16,3072]{3,2,1,0:T(8,128)(2,1)} %courant_ref.7) | copy-start | bytes 2359300
  14.8 8.9 %collective-permute-start.4 = (s16[16,6144]{1,0:T(8,128)(2,1)S(1)}, s16[16,6144]{1,0:T(8,128)(2,1)S(1)}, u32[]{:S(2)}, u32[]{:S(2)}) collective-permute-start(s16[16,6144]{1,0:T(8,128)(2,1)S(1)} %get-tuple-element.30), channel_id=1, source_target_pairs={{0,4},{4,0},{8,12},{12,8},{16,20},{20,16},{24,28},{28,24},{1,5},{5... | collective-permute-start | bytes 589832 | tf_op jit(solution)/shard_map/ppermute | solution.py:595
  23.8 4.4 %copy-start.3 = (bf16[4,1536,256]{2,1,0:T(8,128)(2,1)S(1)}, bf16[4,1536,256]{2,1,0:T(8,128)(2,1)}, u32[]{:S(2)}) copy-start(bf16[4,1536,256]{2,1,0:T(8,128)(2,1)} %constant.48.clone.table_ref) | copy-start | bytes 9437188
  23.8 4.4 %copy-start.8 = (s32[32]{0:T(128)S(1)}, s32[32]{0:T(128)}, u32[]{:S(2)}) copy-start(s32[32]{0:T(128)} %cut_ref.3) | copy-start | bytes 388
  26.1 5.6 %collective-permute-start.5 = (s16[16,6400]{1,0:T(8,128)(2,1)S(1)}, s16[16,6400]{1,0:T(8,128)(2,1)S(1)}, u32[]{:S(2)}, u32[]{:S(2)}) collective-permute-start(s16[16,6400]{1,0:T(8,128)(2,1)S(1)} %get-tuple-element.38), channel_id=1, source_target_pairs={{0,8},{8,0},{4,12},{12,4},{16,24},{24,16},{20,28},{28,20},{1,9},{9... | collective-permute-start | bytes 614408 | tf_op jit(solution)/shard_map/ppermute | solution.py:642
  26.2 6.5 %collective-permute-start.6 = (s16[16,6400]{1,0:T(8,128)(2,1)S(1)}, s16[16,6400]{1,0:T(8,128)(2,1)S(1)}, u32[]{:S(2)}, u32[]{:S(2)}) collective-permute-start(s16[16,6400]{1,0:T(8,128)(2,1)S(1)} %get-tuple-element.39), channel_id=1, source_target_pairs={{8,16},{16,8},{12,20},{20,12},{9,17},{17,9},{13,21},{21,13},{10,18... | collective-permute-start | bytes 614408 | tf_op jit(solution)/shard_map/ppermute | solution.py:643
  32.7 23.8 %copy-start.6 = (f32[64,192]{1,0:T(8,128)S(1)}, f32[64,192]{1,0:T(8,128)}, u32[]{:S(2)}) copy-start(f32[64,192]{1,0:T(8,128)} %constant.49.clone.refs_10_) | copy-start | bytes 147460
  32.7 23.8 %copy-start.7 = (f32[64,64]{1,0:T(8,128)S(1)}, f32[64,64]{1,0:T(8,128)}, u32[]{:S(2)}) copy-start(f32[64,64]{1,0:T(8,128)} %refs_9_.1) | copy-start | bytes 49156
  35.9 9.4 %collective-permute-start.10 = (s16[16,3200]{1,0:T(8,128)(2,1)S(1)}, s16[16,3200]{1,0:T(8,128)(2,1)S(1)}, u32[]{:S(2)}, u32[]{:S(2)}) collective-permute-start(s16[16,3200]{1,0:T(8,128)(2,1)S(1)} %get-tuple-element.44), channel_id=1, source_target_pairs={{0,4},{1,5},{2,6},{3,7},{4,0},{5,1},{6,2},{7,3},{8,12},{9,13},{10,... | collective-permute-start | bytes 307208 | tf_op jit(solution)/shard_map/ppermute | solution.py:675
  37.1 10.1 %collective-permute-start.11 = (s16[16,3200]{1,0:T(8,128)(2,1)S(1)}, s16[16,3200]{1,0:T(8,128)(2,1)S(1)}, u32[]{:S(2)}, u32[]{:S(2)}) collective-permute-start(s16[16,3200]{1,0:T(8,128)(2,1)S(1)} %get-tuple-element.45), channel_id=1, source_target_pairs={{0,5},{1,4},{2,7},{3,6},{4,1},{5,0},{6,3},{7,2},{8,13},{9,12},{10,... | collective-permute-start | bytes 307208 | tf_op jit(solution)/shard_map/ppermute | solution.py:675
  42.5 7.8 %collective-permute-start.12 = (s16[16,3200]{1,0:T(8,128)(2,1)S(1)}, s16[16,3200]{1,0:T(8,128)(2,1)S(1)}, u32[]{:S(2)}, u32[]{:S(2)}) collective-permute-start(s16[16,3200]{1,0:T(8,128)(2,1)S(1)} %get-tuple-element.46), channel_id=1, source_target_pairs={{0,6},{1,7},{2,4},{3,5},{4,2},{5,3},{6,0},{7,1},{8,14},{9,15},{10,... | collective-permute-start | bytes 307208 | tf_op jit(solution)/shard_map/ppermute | solution.py:675
  44.7 7.9 %collective-permute-start.13 = (s16[16,3200]{1,0:T(8,128)(2,1)S(1)}, s16[16,3200]{1,0:T(8,128)(2,1)S(1)}, u32[]{:S(2)}, u32[]{:S(2)}) collective-permute-start(s16[16,3200]{1,0:T(8,128)(2,1)S(1)} %get-tuple-element.47), channel_id=1, source_target_pairs={{0,7},{1,6},{2,5},{3,4},{4,3},{5,2},{6,1},{7,0},{8,15},{9,14},{10,... | collective-permute-start | bytes 307208 | tf_op jit(solution)/shard_map/ppermute | solution.py:675
  45.0 7.6 %collective-permute-start.7 = (s16[16,3200]{1,0:T(8,128)(2,1)S(1)}, s16[16,3200]{1,0:T(8,128)(2,1)S(1)}, u32[]{:S(2)}, u32[]{:S(2)}) collective-permute-start(s16[16,3200]{1,0:T(8,128)(2,1)S(1)} %get-tuple-element.41), channel_id=1, source_target_pairs={{0,1},{1,0},{2,3},{3,2},{4,5},{5,4},{6,7},{7,6},{8,9},{9,8},{10,11... | collective-permute-start | bytes 307208 | tf_op jit(solution)/shard_map/ppermute | solution.py:687
  45.3 8.9 %collective-permute-start.8 = (s16[16,3200]{1,0:T(8,128)(2,1)S(1)}, s16[16,3200]{1,0:T(8,128)(2,1)S(1)}, u32[]{:S(2)}, u32[]{:S(2)}) collective-permute-start(s16[16,3200]{1,0:T(8,128)(2,1)S(1)} %get-tuple-element.42), channel_id=1, source_target_pairs={{0,2},{1,3},{2,0},{3,1},{4,6},{5,7},{6,4},{7,5},{8,10},{9,11},{10,... | collective-permute-start | bytes 307208 | tf_op jit(solution)/shard_map/ppermute | solution.py:687
  47.3 9.2 %collective-permute-start.9 = (s16[16,3200]{1,0:T(8,128)(2,1)S(1)}, s16[16,3200]{1,0:T(8,128)(2,1)S(1)}, u32[]{:S(2)}, u32[]{:S(2)}) collective-permute-start(s16[16,3200]{1,0:T(8,128)(2,1)S(1)} %get-tuple-element.43), channel_id=1, source_target_pairs={{0,3},{1,2},{2,1},{3,0},{4,7},{5,6},{6,5},{7,4},{8,11},{9,10},{10,... | collective-permute-start | bytes 307208 | tf_op jit(solution)/shard_map/ppermute | solution.py:687

commit v3 on v2

--- a/solution.py
+++ b/solution.py
@@ -162,11 +162,9 @@
     width = count * LANE
     lanes = lax.broadcasted_iota(jnp.int32, (z.half, LANE), 1)
 
-    def part(i, carry):
-        at = pl.multiple_of(i * width, LANE)
-
+    def part(at):
         def piece(k):
-            return pl.ds(pl.multiple_of(at + k * LANE, LANE), LANE)
+            return pl.ds(at + k * LANE, LANE)
 
         def row(j, f):
             return [row_of(j, f, piece(k + 1)) for k in range(count)]
@@ -207,9 +205,9 @@
                     above = row(j + 4, f)
                     rows = rows[1:] + [above]
                     sums = sums[1:] + [[a + b for a, b in zip(rows[2], rows[3])]]
-        return carry
-
-    lax.fori_loop(0, z.lon // width, part, 0)
+
+    for i in range(z.lon // width):
+        part(i * width)
 
 
 def filter_tables(lon):
@@ -296,21 +294,19 @@
 
 
 def faces(z, cx_ref, cy_ref, winds_ref):
-    def face_rows(j, carry):
-        wind = cx_ref[j] * (1.0 / 24.0)
-        here = wind[:, LANE : LANE + z.lon]
-        winds_ref[j] = here + pltpu.roll(wind, z.pad - 1, 1)[:, LANE : LANE + z.lon]
-        winds_ref[z.rows + j] = here + pltpu.roll(wind, 1, 1)[:, LANE : LANE + z.lon]
-        return carry
-
-    lax.fori_loop(0, z.rows, face_rows, 0)
+    lanes = lax.broadcasted_iota(jnp.int32, (z.half, LANE), 1)
+    for j in range(z.rows):
+        pieces = [cx_ref[j, :, i : i + LANE] * (1.0 / 24.0) for i in range(0, z.pad, LANE)]
+        for out, shift in ((j, 1), (z.rows + j, -1)):
+            for k, moved in enumerate(shifted(pieces, shift, lanes)):
+                winds_ref[out, :, k * LANE : (k + 1) * LANE] = pieces[k + 1] + moved
     for j in range(z.rows + 1):
         winds_ref[2 * z.rows + j] = (cy_ref[j] + cy_ref[j + 1]) * (1.0 / 24.0)
 
 
 def writer(new_ref):
     def write(row, f, at, k, values):
-        new_ref[row, f, :, pl.ds(pl.multiple_of(at + (k + 1) * LANE, LANE), LANE)] = values
+        new_ref[row, f, :, pl.ds(at + (k + 1) * LANE, LANE)] = values
 
     return write
 
@@ -431,7 +427,7 @@
     ):
 
         def keep(row, f, at, k, values):
-            inner_ref[2 * i + row, f, :, pl.ds(pl.multiple_of(at + k * LANE, LANE), LANE)] = values
+            inner_ref[2 * i + row, f, :, pl.ds(at + k * LANE, LANE)] = values
 
         substep(z, 2, base, lambda j, f, piece: new_ref[low + j, f, :, piece], winds_ref, keep)
 
@@ -473,7 +469,7 @@
         v_ref[2 * (1 - side) + r] = inner_ref[inner_at + r]
 
     def write(row, f, at, k, values):
-        v_ref[2 * side + row, f, :, pl.ds(pl.multiple_of(at + k * LANE, LANE), LANE)] = values
+        v_ref[2 * side + row, f, :, pl.ds(at + k * LANE, LANE)] = values
 
     substep(z, 2, 2 * side, lambda j, f, piece: u_ref[j, f, :, piece], winds_ref, write)
 
@@ -495,18 +491,18 @@
         refs[-1][i] = decoder(ref[:, at : at + LANE])
 
 
-def column_kernel(z, parts, par_ref, *refs):
+def column_kernel(z, parts, far, par_ref, *refs):
     got, (scales_ref, remap_ref, upward_ref, surface_ref, out_ref, geo_ref, x_ref) = refs[: 2 * parts], refs[2 * parts :]
     p, lev = par_ref[0], par_ref[2]
     column = out_ref.shape[-1]
     at = pl.multiple_of(pl.program_id(0) * column, LANE)
     for i, ref in enumerate(got):
-        side = p if i < parts else 1 - p
+        side = 1 - p if i < parts else p
         s = jnp.bitwise_xor(lev, i % parts)
-        if i < parts:
+        if i in far:
+            scale = scales_ref[far.index(i)]
+        else:
             scale = decoder(ref[:, z.rows * column : z.rows * column + LANE])
-        else:
-            scale = scales_ref[i - parts]
         codes = ref[:, pl.ds(at, column)].astype(jnp.int32).astype(jnp.float32)
         values = codes * tiled(scale, column)
         level = pl.multiple_of(s * z.levels + side * z.half, z.half)
@@ -668,30 +664,29 @@
         cost_estimate=cost(),
     )(place, cutoffs, new, inner, own_winds, other_winds, one, two, tables)
     got = []
-    for b, block in enumerate(blocks[:parts]):
+    for i, block in enumerate(blocks):
+        b, across = i % parts, int(i < parts)
         pairs = [
-            (i * parts + j, (i ^ 1) * parts + (j ^ b)) for i in range(lats) for j in range(parts)
+            (k * parts + j, (k ^ across) * parts + (j ^ b)) for k in range(lats) for j in range(parts)
         ]
-        got.append(lax.ppermute(block, ("lat", "lev"), pairs))
+        got.append(lax.ppermute(block, ("lat", "lev"), pairs) if i != parts else block)
+    far = [i for i in range(2 * parts) if i % parts >= parts // 2]
     scales = pl.pallas_call(
         functools.partial(scale_kernel, rows * column),
         name="scales",
-        in_specs=[whole()] * parts,
+        in_specs=[whole()] * len(far),
         out_specs=whole(),
-        out_shape=shape(parts, tall, LANE),
+        out_shape=shape(len(far), tall, LANE),
         compiler_params=params(),
         cost_estimate=cost(),
-    )(*got)
-    for b, block in enumerate(blocks[parts:]):
-        pairs = [(j, j ^ b) for j in range(parts)]
-        got.insert(b, lax.ppermute(block, "lev", pairs) if b else block)
+    )(*[got[i] for i in far])
 
     count = remap_weights.shape[0]
     upward = np.triu(np.ones((count, count), np.float32), 1) + 0.5 * np.eye(count, dtype=np.float32)
     upward = jnp.asarray(np.concatenate([upward, 0.0 * upward, upward], axis=1))
     surface = lax.dynamic_slice_in_dim(surface, lev * column, column, 1)
     remapped, geopotential = pl.pallas_call(
-        functools.partial(column_kernel, z, parts),
+        functools.partial(column_kernel, z, parts, far),
         name="columns",
         grid=(rows,),
         in_specs=[scalars()]

time: 60.8 us -> 56.4 us (0.928); the launches traced: 59.7 us -> 56.2 us
  Pallas kernels: 18.7 us -> 15.3 us
  starting transfers between devices: 20.6 us -> 18.1 us
  waiting for transfers between devices: 16.9 us -> 19.3 us
    ppermute x7, starting transfers between devices: 12.4 us -> 9.92 us  [shards(): lax.ppermute(block, ('lat', 'lev'), pairs)]
    pallas_call x1, Pallas kernels: 3.56 us -> 2.32 us  [shards(): pl.pallas_call(functools.partial(inner_kernel, z), name='inner', in_specs...]
    ppermute x7, waiting for transfers between devices: 8.17 us -> 9.32 us  [shards(): lax.ppermute(block, ('lat', 'lev'), pairs)]
    ppermute x1, waiting for transfers between devices: 0.94 us -> 1.91 us  [shards(): two = lax.ppermute(two_code, 'lat', twos)]
    pallas_call x1, Pallas kernels: 3.19 us -> 2.38 us  [shards(): pl.pallas_call(functools.partial(outer_kernel, z, parts), name='outer', i...]
    pallas_call x1, Pallas kernels: 2.28 us -> 1.6 us  [shards(): pl.pallas_call(functools.partial(other_kernel, z), name='other', in_specs...]
    pallas_call x1, Pallas kernels: 2.98 us -> 2.32 us  [shards(): pl.pallas_call(functools.partial(own_kernel, z), name='own', in_specs=[sc...]
  transfers between devices with their start and end apart: 14 -> 14, of which waited for: 10 -> 10; matrix products, arithmetic and copies ran while one was open for 0% -> 0% of each run, Pallas kernels for 14% -> 11%
where the time goes in v3:
time: 56.4 us; the launch traced here: 56.2 us
  waiting for transfers between devices  19.3 us (34%)
  starting transfers between devices  18.1 us (32%)
  Pallas kernels  15.3 us (27%)
  local copies, waits for them, and re-layouts  2.6 us (5%)
  between operations  0.81 us (1%)
    ppermute x7, starting transfers between devices, shards(): lax.ppermute(block, ('lat', 'lev'), pairs)  9.92 us
    ppermute x7, waiting for transfers between devices, shards(): lax.ppermute(block, ('lat', 'lev'), pairs)  9.32 us
    pallas_call x1, Pallas kernels, shards(): pl.pallas_call(functools.partial(column_kernel, z, parts, far), name='col...  3.16 us
    ppermute x1, waiting for transfers between devices, shards(): two = lax.ppermute(two, 'lat', twos)  3.15 us
    ppermute x1, waiting for transfers between devices, shards(): edge = lax.ppermute(edge, 'lat', swap)  3.14 us
    unnamed x18, local copies, waits for them, and re-layouts  2.58 us
    pallas_call x1, Pallas kernels, shards(): pl.pallas_call(functools.partial(outer_kernel, z, parts), name='outer', i...  2.38 us
    pallas_call x1, Pallas kernels, shards(): pl.pallas_call(functools.partial(own_kernel, z), name='own', in_specs=[sc...  2.32 us
  transfers between devices with their start and end apart: 14, of which 10 were waited for; matrix products, arithmetic and copies ran while one was open for 0% of the time, Pallas kernels for 11%

profile of v3, /device:TPU:17, one launch (start us, length us, event | category | flops | bytes accessed | tf_op | source)
XLA Modules:
  0.0 56.2 jit_solution(14388946031919739875)
XLA Ops:
  0.6 0.0 copy-start
  0.6 2.0 %edge.1 = s16[16,9472]{1,0:T(8,128)(2,1)} custom-call(f32[2,4,16,3072]{3,2,1,0:T(8,128)} %fields_ref.5, bf16[2,4,16,3072]{3,2,1,0:T(8,128)(2,1)} %courant_ref.7), custom_call_target="tpu_custom_call" | custom-call | flops 1000 | bytes 1000 | tf_op jit(solution)/shard_map/edge/pallas_call | solution.py:566
  2.6 1.3 %collective-permute-start = (s16[16,9472]{1,0:T(8,128)(2,1)}, s16[16,9472]{1,0:T(8,128)(2,1)S(1)}, u32[]{:S(2)}, u32[]{:S(2)}) collective-permute-start(s16[16,9472]{1,0:T(8,128)(2,1)} %edge.1), channel_id=1, source_target_pairs={{0,4},{4,0},{8,12},{12,8},{16,20},{20,16},{24,28},{28,24},{1,5},{5... | collective-permute-start | bytes 909320 | tf_op jit(solution)/shard_map/ppermute | solution.py:580
  3.9 0.1 pad_add_fusion.par_ref
  4.0 1.4 %copy-done.1 = f32[2,4,16,3072]{3,2,1,0:T(8,128)S(1)} copy-done((f32[2,4,16,3072]{3,2,1,0:T(8,128)S(1)}, f32[2,4,16,3072]{3,2,1,0:T(8,128)}, u32[]{:S(2)}) %copy-start.1) | copy-done | bytes 1572888
  5.4 1.1 %copy-done.4 = bf16[2,4,16,3072]{3,2,1,0:T(8,128)(2,1)S(1)} copy-done((bf16[2,4,16,3072]{3,2,1,0:T(8,128)(2,1)S(1)}, bf16[2,4,16,3072]{3,2,1,0:T(8,128)(2,1)}, u32[]{:S(2)}) %copy-start.4) | copy-done | bytes 786456
  6.5 1.0 %rest.1 = (s16[16,9472]{1,0:T(8,128)(2,1)S(1)}, s16[16,6144]{1,0:T(8,128)(2,1)S(1)}, s16[16,9472]{1,0:T(8,128)(2,1)S(1)}) custom-call(s32[4]{0:T(128)S(1)} %pad_add_fusion.par_ref, f32[2,4,16,3072]{3,2,1,0:T(8,128)S(1)} %copy-done.1, bf16[2,4,16,3072]{3,2,1,0:T(8,128)(2,1)S(1)} %copy-done.4), custom_call_target="tpu_custom_call" | custom-call | flops 1000 | bytes 1000 | tf_op jit(solution)/shard_map/rest/pallas_call | solution.py:581
  7.5 0.3 collective-permute-start.1
  7.8 3.1 %collective-permute-done.edge_ref = s16[16,9472]{1,0:T(8,128)(2,1)S(1)} collective-permute-done((s16[16,9472]{1,0:T(8,128)(2,1)}, s16[16,9472]{1,0:T(8,128)(2,1)S(1)}, u32[]{:S(2)}, u32[]{:S(2)}) %collective-permute-start) | collective-permute-done | bytes 303136 | tf_op jit(solution)/shard_map/ppermute | solution.py:580
  11.0 0.6 %pick.1 = (s16[16,9472]{1,0:T(8,128)(2,1)S(1)}, s16[16,9472]{1,0:T(8,128)(2,1)S(1)}) custom-call(s32[4]{0:T(128)S(1)} %pad_add_fusion.par_ref, s16[16,9472]{1,0:T(8,128)(2,1)S(1)} %get-tuple-element.26.own_ref, s16[16,9472]{1,0:T(8,128)(2,1)S(1)} %collective-permute-done.edge_ref), custom_call_target="tpu_custom_call" | custom-call | flops 1000 | bytes 1000 | tf_op jit(solution)/shard_map/pick/pallas_call | solution.py:592
  11.5 1.4 %collective-permute-start.2 = (s16[16,9472]{1,0:T(8,128)(2,1)S(1)}, s16[16,9472]{1,0:T(8,128)(2,1)S(1)}, u32[]{:S(2)}, u32[]{:S(2)}) collective-permute-start(s16[16,9472]{1,0:T(8,128)(2,1)S(1)} %get-tuple-element.27), channel_id=1, source_target_pairs={{0,8},{8,0},{4,12},{12,4},{16,24},{24,16},{20,28},{28,20},{1,9},{9... | collective-permute-start | bytes 909320 | tf_op jit(solution)/shard_map/ppermute | solution.py:601
  12.9 1.9 %collective-permute-start.3 = (s16[16,9472]{1,0:T(8,128)(2,1)S(1)}, s16[16,9472]{1,0:T(8,128)(2,1)S(1)}, u32[]{:S(2)}, u32[]{:S(2)}) collective-permute-start(s16[16,9472]{1,0:T(8,128)(2,1)S(1)} %get-tuple-element.28), channel_id=1, source_target_pairs={{8,16},{16,8},{12,20},{20,12},{9,17},{17,9},{13,21},{21,13},{10,18... | collective-permute-start | bytes 909320 | tf_op jit(solution)/shard_map/ppermute | solution.py:602
  14.8 0.0 copy-start.5
  14.8 1.3 %collective-permute-start.4 = (s16[16,6144]{1,0:T(8,128)(2,1)S(1)}, s16[16,6144]{1,0:T(8,128)(2,1)S(1)}, u32[]{:S(2)}, u32[]{:S(2)}) collective-permute-start(s16[16,6144]{1,0:T(8,128)(2,1)S(1)} %get-tuple-element.30), channel_id=1, source_target_pairs={{0,4},{4,0},{8,12},{12,8},{16,20},{20,16},{24,28},{28,24},{1,5},{5... | collective-permute-start | bytes 589832 | tf_op jit(solution)/shard_map/ppermute | solution.py:591
  16.1 1.3 %collective-permute-done.1.middle_ref = s16[16,9472]{1,0:T(8,128)(2,1)S(1)} collective-permute-done((s16[16,9472]{1,0:T(8,128)(2,1)S(1)}, s16[16,9472]{1,0:T(8,128)(2,1)S(1)}, u32[]{:S(2)}, u32[]{:S(2)}) %collective-permute-start.1) | collective-permute-done | bytes 303136 | tf_op jit(solution)/shard_map/ppermute | solution.py:590
  17.4 0.1 collective-permute-done.2.one_ref
  17.6 3.2 %collective-permute-done.3.two_ref = s16[16,9472]{1,0:T(8,128)(2,1)S(1)} collective-permute-done((s16[16,9472]{1,0:T(8,128)(2,1)S(1)}, s16[16,9472]{1,0:T(8,128)(2,1)S(1)}, u32[]{:S(2)}, u32[]{:S(2)}) %collective-permute-start.3) | collective-permute-done | bytes 303136 | tf_op jit(solution)/shard_map/ppermute | solution.py:602
  20.7 0.0 copy-done.2
  20.8 2.3 %own.1 = (f32[4,2,8,3328]{3,2,1,0:T(8,128)S(1)}, f32[13,8,3072]{2,1,0:T(8,128)S(1)}, s16[16,6400]{1,0:T(8,128)(2,1)S(1)}, f32[12,2,8,3328]{3,2,1,0:T(8,128)S(1)}) custom-call(s32[4]{0:T(128)S(1)} %pad_add_fusion.par_ref, f32[2,4,16,3072]{3,2,1,0:T(8,128)S(1)} %copy-done.2, bf16[2,4,16,3072]{3,2,1,0:T(8,128)(2,1)S(1)} %copy-done.4, ...), custom_call_target="tpu_custom_call" | custom-call | flops 1000 | bytes 1000 | tf_op jit(solution)/shard_map/own/pallas_call | solution.py:608
  23.1 0.0 collective-permute-done.4.last_ref
  23.1 0.0 copy-done.5
  23.1 0.0 copy-start.3
  23.1 0.0 copy-start.8
  23.1 1.6 %other.1 = (f32[2,2,8,3328]{3,2,1,0:T(8,128)S(1)}, f32[13,8,3072]{2,1,0:T(8,128)S(1)}, s16[16,6400]{1,0:T(8,128)(2,1)S(1)}, s16[16,6400]{1,0:T(8,128)(2,1)S(1)}) custom-call(s32[4]{0:T(128)S(1)} %pad_add_fusion.par_ref, bf16[2,4,16,3072]{3,2,1,0:T(8,128)(2,1)S(1)} %copy-done.5, s16[16,9472]{1,0:T(8,128)(2,1)S(1)} %collective-permute-done.edge_ref, ...), custom_call_target="tpu_custom_call" | custom-call | flops 1000 | bytes 1000 | tf_op jit(solution)/shard_map/other/pallas_call | solution.py:623
  24.7 0.1 collective-permute-start.5
  24.8 1.9 %collective-permute-start.6 = (s16[16,6400]{1,0:T(8,128)(2,1)S(1)}, s16[16,6400]{1,0:T(8,128)(2,1)S(1)}, u32[]{:S(2)}, u32[]{:S(2)}) collective-permute-start(s16[16,6400]{1,0:T(8,128)(2,1)S(1)} %get-tuple-element.39), channel_id=1, source_target_pairs={{8,16},{16,8},{12,20},{20,12},{9,17},{17,9},{13,21},{21,13},{10,18... | collective-permute-start | bytes 614408 | tf_op jit(solution)/shard_map/ppermute | solution.py:639
  26.8 0.0 copy-done.3
  26.8 0.0 copy-done.8
  26.8 2.3 %inner.1 = (f32[8,2,8,3328]{3,2,1,0:T(8,128)S(1)}, f32[4,2,8,3072]{3,2,1,0:T(8,128)S(1)}) custom-call(s32[4]{0:T(128)S(1)} %pad_add_fusion.par_ref, s32[32]{0:T(128)S(1)} %copy-done.8, f32[4,2,8,3328]{3,2,1,0:T(8,128)S(1)} %get-tuple-element.29.own_ref, f32[2,2,8,3328]{3,2,1,0:T(8,128)S(1)} %get-tuple-element.33.other_ref, ...), custom_call_target="tpu_custom_call" | custom-call | flops 1000 | bytes 1000 | tf_op jit(solution)/shard_map/inner/pallas_call | solution.py:642
  29.1 0.3 collective-permute-done.5.one_ref
  29.4 1.9 %collective-permute-done.6.two_ref = s16[16,6400]{1,0:T(8,128)(2,1)S(1)} collective-permute-done((s16[16,6400]{1,0:T(8,128)(2,1)S(1)}, s16[16,6400]{1,0:T(8,128)(2,1)S(1)}, u32[]{:S(2)}, u32[]{:S(2)}) %collective-permute-start.6) | collective-permute-done | bytes 204832 | tf_op jit(solution)/shard_map/ppermute | solution.py:639
  31.3 2.4 %outer.1 = (s16[16,3200]{1,0:T(8,128)(2,1)S(1)}, s16[16,3200]{1,0:T(8,128)(2,1)S(1)}, s16[16,3200]{1,0:T(8,128)(2,1)S(1)}, s16[16,3200]{1,0:T(8,128)(2,1)S(1)}, ...) custom-call(s32[4]{0:T(128)S(1)} %pad_add_fusion.par_ref, ...), custom_call_target="tpu_custom_call" | custom-call | flops 1000 | bytes 1000 | tf_op jit(solution)/shard_map/outer/pallas_call | solution.py:653
  33.7 7.1 %collective-permute-start.10 = (s16[16,3200]{1,0:T(8,128)(2,1)S(1)}, s16[16,3200]{1,0:T(8,128)(2,1)S(1)}, u32[]{:S(2)}, u32[]{:S(2)}) collective-permute-start(s16[16,3200]{1,0:T(8,128)(2,1)S(1)} %get-tuple-element.43), channel_id=1, source_target_pairs={{0,7},{1,6},{2,5},{3,4},{4,3},{5,2},{6,1},{7,0},{8,15},{9,14},{10,... | collective-permute-start | bytes 307208 | tf_op jit(solution)/shard_map/ppermute | solution.py:672
  40.8 0.2 collective-permute-start.12
  41.0 0.0 collective-permute-start.13
  41.0 1.6 %collective-permute-start.9 = (s16[16,3200]{1,0:T(8,128)(2,1)S(1)}, s16[16,3200]{1,0:T(8,128)(2,1)S(1)}, u32[]{:S(2)}, u32[]{:S(2)}) collective-permute-start(s16[16,3200]{1,0:T(8,128)(2,1)S(1)} %get-tuple-element.42), channel_id=1, source_target_pairs={{0,6},{1,7},{2,4},{3,5},{4,2},{5,3},{6,0},{7,1},{8,14},{9,15},{10,... | collective-permute-start | bytes 307208 | tf_op jit(solution)/shard_map/ppermute | solution.py:672
  42.6 0.5 collective-permute-start.11
  43.1 1.2 %collective-permute-done.10.refs_1_.refs_3_ = s16[16,3200]{1,0:T(8,128)(2,1)S(1)} collective-permute-done((s16[16,3200]{1,0:T(8,128)(2,1)S(1)}, s16[16,3200]{1,0:T(8,128)(2,1)S(1)}, u32[]{:S(2)}, u32[]{:S(2)}) %collective-permute-start.10) | collective-permute-done | bytes 102432 | tf_op jit(solution)/shard_map/ppermute | solution.py:672
  44.4 0.0 collective-permute-start.7
  44.4 4.5 %collective-permute-done.12.refs_2_.refs_6_ = s16[16,3200]{1,0:T(8,128)(2,1)S(1)} collective-permute-done((s16[16,3200]{1,0:T(8,128)(2,1)S(1)}, s16[16,3200]{1,0:T(8,128)(2,1)S(1)}, u32[]{:S(2)}, u32[]{:S(2)}) %collective-permute-start.12) | collective-permute-done | bytes 102432 | tf_op jit(solution)/shard_map/ppermute | solution.py:672
  48.9 0.5 collective-permute-start.8
  49.4 0.0 copy-done
  49.4 1.0 %collective-permute-done.13.refs_3_.refs_7_ = s16[16,3200]{1,0:T(8,128)(2,1)S(1)} collective-permute-done((s16[16,3200]{1,0:T(8,128)(2,1)S(1)}, s16[16,3200]{1,0:T(8,128)(2,1)S(1)}, u32[]{:S(2)}, u32[]{:S(2)}) %collective-permute-start.13) | collective-permute-done | bytes 102432 | tf_op jit(solution)/shard_map/ppermute | solution.py:672
  50.4 0.0 collective-permute-done.9.refs_0_.refs_2_
  50.5 0.0 collective-permute-done.11.refs_5_
  50.5 0.0 collective-permute-done.7.refs_0_
  50.5 2.5 %collective-permute-done.8.refs_1_ = s16[16,3200]{1,0:T(8,128)(2,1)S(1)} collective-permute-done((s16[16,3200]{1,0:T(8,128)(2,1)S(1)}, s16[16,3200]{1,0:T(8,128)(2,1)S(1)}, u32[]{:S(2)}, u32[]{:S(2)}) %collective-permute-start.8) | collective-permute-done | bytes 102432 | tf_op jit(solution)/shard_map/ppermute | solution.py:672
  53.0 3.2 %columns.1 = (f32[2,4,64,768]{3,2,1,0:T(8,128)}, f32[4,64,768]{2,1,0:T(8,128)}) custom-call(s32[4]{0:T(128)S(1)} %pad_add_fusion.par_ref, s16[16,3200]{1,0:T(8,128)(2,1)S(1)} %collective-permute-done.7.refs_0_, s16[16,3200]{1,0:T(8,128)(2,1)S(1)} %collective-permute-done.8.refs_1_, s16[16,3200]{1,0:T(8,128)(2,1)S(1)} %collective-permute-done.9.refs_0_.refs_2_, ...), custom_call_target="tpu_custom_call" | custom-call | flops 1000 | bytes 1000 | tf_op jit(solution)/shard_map/columns/pallas_call | solution.py:688
  (10 shorter events, 0.0 us)
Async XLA Ops:
  0.6 48.8 %copy-start = (f32[4,3072]{1,0:T(4,128)S(1)}, f32[4,3072]{1,0:T(4,128)}, u32[]{:S(2)}) copy-start(f32[4,3072]{1,0:T(4,128)} %param.10) | copy-start | bytes 147460
  2.6 8.3 %collective-permute-start = (s16[16,9472]{1,0:T(8,128)(2,1)}, s16[16,9472]{1,0:T(8,128)(2,1)S(1)}, u32[]{:S(2)}, u32[]{:S(2)}) collective-permute-start(s16[16,9472]{1,0:T(8,128)(2,1)} %edge.1), channel_id=1, source_target_pairs={{0,4},{4,0},{8,12},{12,8},{16,20},{20,16},{24,28},{28,24},{1,5},{5... | collective-permute-start | bytes 909320 | tf_op jit(solution)/shard_map/ppermute | solution.py:580
  4.0 1.4 %copy-start.1 = (f32[2,4,16,3072]{3,2,1,0:T(8,128)S(1)}, f32[2,4,16,3072]{3,2,1,0:T(8,128)}, u32[]{:S(2)}) copy-start(f32[2,4,16,3072]{3,2,1,0:T(8,128)} %fields_ref.5) | copy-start | bytes 4718596
  5.4 1.1 %copy-start.4 = (bf16[2,4,16,3072]{3,2,1,0:T(8,128)(2,1)S(1)}, bf16[2,4,16,3072]{3,2,1,0:T(8,128)(2,1)}, u32[]{:S(2)}) copy-start(bf16[2,4,16,3072]{3,2,1,0:T(8,128)(2,1)} %courant_ref.7) | copy-start | bytes 2359300
  6.5 14.2 %copy-start.2 = (f32[2,4,16,3072]{3,2,1,0:T(8,128)S(1)}, f32[2,4,16,3072]{3,2,1,0:T(8,128)}, u32[]{:S(2)}) copy-start(f32[2,4,16,3072]{3,2,1,0:T(8,128)} %fields_ref.5) | copy-start | bytes 4718596
  7.5 10.0 %collective-permute-start.1 = (s16[16,9472]{1,0:T(8,128)(2,1)S(1)}, s16[16,9472]{1,0:T(8,128)(2,1)S(1)}, u32[]{:S(2)}, u32[]{:S(2)}) collective-permute-start(s16[16,9472]{1,0:T(8,128)(2,1)S(1)} %get-tuple-element.25), channel_id=1, source_target_pairs={{0,4},{4,0},{8,12},{12,8},{16,20},{20,16},{24,28},{28,24},{1,5},{5... | collective-permute-start | bytes 909320 | tf_op jit(solution)/shard_map/ppermute | solution.py:590
  11.5 6.0 %collective-permute-start.2 = (s16[16,9472]{1,0:T(8,128)(2,1)S(1)}, s16[16,9472]{1,0:T(8,128)(2,1)S(1)}, u32[]{:S(2)}, u32[]{:S(2)}) collective-permute-start(s16[16,9472]{1,0:T(8,128)(2,1)S(1)} %get-tuple-element.27), channel_id=1, source_target_pairs={{0,8},{8,0},{4,12},{12,4},{16,24},{24,16},{20,28},{28,20},{1,9},{9... | collective-permute-start | bytes 909320 | tf_op jit(solution)/shard_map/ppermute | solution.py:601
  12.9 7.8 %collective-permute-start.3 = (s16[16,9472]{1,0:T(8,128)(2,1)S(1)}, s16[16,9472]{1,0:T(8,128)(2,1)S(1)}, u32[]{:S(2)}, u32[]{:S(2)}) collective-permute-start(s16[16,9472]{1,0:T(8,128)(2,1)S(1)} %get-tuple-element.28), channel_id=1, source_target_pairs={{8,16},{16,8},{12,20},{20,12},{9,17},{17,9},{13,21},{21,13},{10,18... | collective-permute-start | bytes 909320 | tf_op jit(solution)/shard_map/ppermute | solution.py:602
  14.8 8.3 %copy-start.5 = (bf16[2,4,16,3072]{3,2,1,0:T(8,128)(2,1)S(1)}, bf16[2,4,16,3072]{3,2,1,0:T(8,128)(2,1)}, u32[]{:S(2)}) copy-start(bf16[2,4,16,3072]{3,2,1,0:T(8,128)(2,1)} %courant_ref.7) | copy-start | bytes 2359300
  14.8 8.2 %collective-permute-start.4 = (s16[16,6144]{1,0:T(8,128)(2,1)S(1)}, s16[16,6144]{1,0:T(8,128)(2,1)S(1)}, u32[]{:S(2)}, u32[]{:S(2)}) collective-permute-start(s16[16,6144]{1,0:T(8,128)(2,1)S(1)} %get-tuple-element.30), channel_id=1, source_target_pairs={{0,4},{4,0},{8,12},{12,8},{16,20},{20,16},{24,28},{28,24},{1,5},{5... | collective-permute-start | bytes 589832 | tf_op jit(solution)/shard_map/ppermute | solution.py:591
  23.1 3.7 %copy-start.3 = (bf16[4,1536,256]{2,1,0:T(8,128)(2,1)S(1)}, bf16[4,1536,256]{2,1,0:T(8,128)(2,1)}, u32[]{:S(2)}) copy-start(bf16[4,1536,256]{2,1,0:T(8,128)(2,1)} %constant.48.clone.table_ref) | copy-start | bytes 9437188
  23.1 3.7 %copy-start.8 = (s32[32]{0:T(128)S(1)}, s32[32]{0:T(128)}, u32[]{:S(2)}) copy-start(s32[32]{0:T(128)} %cut_ref.3) | copy-start | bytes 388
  24.7 4.7 %collective-permute-start.5 = (s16[16,6400]{1,0:T(8,128)(2,1)S(1)}, s16[16,6400]{1,0:T(8,128)(2,1)S(1)}, u32[]{:S(2)}, u32[]{:S(2)}) collective-permute-start(s16[16,6400]{1,0:T(8,128)(2,1)S(1)} %get-tuple-element.38), channel_id=1, source_target_pairs={{0,8},{8,0},{4,12},{12,4},{16,24},{24,16},{20,28},{28,20},{1,9},{9... | collective-permute-start | bytes 614408 | tf_op jit(solution)/shard_map/ppermute | solution.py:638
  24.8 6.5 %collective-permute-start.6 = (s16[16,6400]{1,0:T(8,128)(2,1)S(1)}, s16[16,6400]{1,0:T(8,128)(2,1)S(1)}, u32[]{:S(2)}, u32[]{:S(2)}) collective-permute-start(s16[16,6400]{1,0:T(8,128)(2,1)S(1)} %get-tuple-element.39), channel_id=1, source_target_pairs={{8,16},{16,8},{12,20},{20,12},{9,17},{17,9},{13,21},{21,13},{10,18... | collective-permute-start | bytes 614408 | tf_op jit(solution)/shard_map/ppermute | solution.py:639
  31.3 21.7 %copy-start.6 = (f32[64,192]{1,0:T(8,128)S(1)}, f32[64,192]{1,0:T(8,128)}, u32[]{:S(2)}) copy-start(f32[64,192]{1,0:T(8,128)} %constant.49.clone.refs_10_) | copy-start | bytes 147460
  31.3 21.7 %copy-start.7 = (f32[64,64]{1,0:T(8,128)S(1)}, f32[64,64]{1,0:T(8,128)}, u32[]{:S(2)}) copy-start(f32[64,64]{1,0:T(8,128)} %refs_9_.1) | copy-start | bytes 49156
  33.7 10.7 %collective-permute-start.10 = (s16[16,3200]{1,0:T(8,128)(2,1)S(1)}, s16[16,3200]{1,0:T(8,128)(2,1)S(1)}, u32[]{:S(2)}, u32[]{:S(2)}) collective-permute-start(s16[16,3200]{1,0:T(8,128)(2,1)S(1)} %get-tuple-element.43), channel_id=1, source_target_pairs={{0,7},{1,6},{2,5},{3,4},{4,3},{5,2},{6,1},{7,0},{8,15},{9,14},{10,... | collective-permute-start | bytes 307208 | tf_op jit(solution)/shard_map/ppermute | solution.py:672
  40.8 8.1 %collective-permute-start.12 = (s16[16,3200]{1,0:T(8,128)(2,1)S(1)}, s16[16,3200]{1,0:T(8,128)(2,1)S(1)}, u32[]{:S(2)}, u32[]{:S(2)}) collective-permute-start(s16[16,3200]{1,0:T(8,128)(2,1)S(1)} %get-tuple-element.46), channel_id=1, source_target_pairs={{0,2},{1,3},{2,0},{3,1},{4,6},{5,7},{6,4},{7,5},{8,10},{9,11},{10,... | collective-permute-start | bytes 307208 | tf_op jit(solution)/shard_map/ppermute | solution.py:672
  41.0 9.4 %collective-permute-start.13 = (s16[16,3200]{1,0:T(8,128)(2,1)S(1)}, s16[16,3200]{1,0:T(8,128)(2,1)S(1)}, u32[]{:S(2)}, u32[]{:S(2)}) collective-permute-start(s16[16,3200]{1,0:T(8,128)(2,1)S(1)} %get-tuple-element.47), channel_id=1, source_target_pairs={{0,3},{1,2},{2,1},{3,0},{4,7},{5,6},{6,5},{7,4},{8,11},{9,10},{10,... | collective-permute-start | bytes 307208 | tf_op jit(solution)/shard_map/ppermute | solution.py:672
  41.0 9.4 %collective-permute-start.9 = (s16[16,3200]{1,0:T(8,128)(2,1)S(1)}, s16[16,3200]{1,0:T(8,128)(2,1)S(1)}, u32[]{:S(2)}, u32[]{:S(2)}) collective-permute-start(s16[16,3200]{1,0:T(8,128)(2,1)S(1)} %get-tuple-element.42), channel_id=1, source_target_pairs={{0,6},{1,7},{2,4},{3,5},{4,2},{5,3},{6,0},{7,1},{8,14},{9,15},{10,... | collective-permute-start | bytes 307208 | tf_op jit(solution)/shard_map/ppermute | solution.py:672
  42.6 7.8 %collective-permute-start.11 = (s16[16,3200]{1,0:T(8,128)(2,1)S(1)}, s16[16,3200]{1,0:T(8,128)(2,1)S(1)}, u32[]{:S(2)}, u32[]{:S(2)}) collective-permute-start(s16[16,3200]{1,0:T(8,128)(2,1)S(1)} %get-tuple-element.45), channel_id=1, source_target_pairs={{0,1},{1,0},{2,3},{3,2},{4,5},{5,4},{6,7},{7,6},{8,9},{9,8},{10,11... | collective-permute-start | bytes 307208 | tf_op jit(solution)/shard_map/ppermute | solution.py:672
  44.4 6.1 %collective-permute-start.7 = (s16[16,3200]{1,0:T(8,128)(2,1)S(1)}, s16[16,3200]{1,0:T(8,128)(2,1)S(1)}, u32[]{:S(2)}, u32[]{:S(2)}) collective-permute-start(s16[16,3200]{1,0:T(8,128)(2,1)S(1)} %get-tuple-element.40), channel_id=1, source_target_pairs={{0,4},{1,5},{2,6},{3,7},{4,0},{5,1},{6,2},{7,3},{8,12},{9,13},{10,... | collective-permute-start | bytes 307208 | tf_op jit(solution)/shard_map/ppermute | solution.py:672
  48.9 4.1 %collective-permute-start.8 = (s16[16,3200]{1,0:T(8,128)(2,1)S(1)}, s16[16,3200]{1,0:T(8,128)(2,1)S(1)}, u32[]{:S(2)}, u32[]{:S(2)}) collective-permute-start(s16[16,3200]{1,0:T(8,128)(2,1)S(1)} %get-tuple-element.41), channel_id=1, source_target_pairs={{0,5},{1,4},{2,7},{3,6},{4,1},{5,0},{6,3},{7,2},{8,13},{9,12},{10,... | collective-permute-start | bytes 307208 | tf_op jit(solution)/shard_map/ppermute | solution.py:672
